TPU v7x, 256 devices: a whole 4x4x8 slice. The times are simulated.
256 devices in a mesh: dp: 32 (over x, y, core), mp: 8 (over z).
Axes of the slice: x: 4, y: 4, z: 8, core: 2. Of those that a mesh axis runs over, the one named last changes fastest.
Arguments:
- residual: bfloat16 [4096, 4096], P('dp', 'mp'), may hold values from -6 to 6
- queries: bfloat16 [4096, 4096], P('dp', 'mp'), may hold values from -36 to 36
- key_rows: bfloat16 [4096, 4096], P('dp', 'mp'), may hold values from -36 to 36
- value_rows: bfloat16 [4096, 4096], P('dp', 'mp'), may hold values from -6 to 6
- lengths: int32 [32, 4], P('dp'), may hold values from 1 to 64, 128 in all within a row
- labels: int32 [4096, 1], P('dp'), may hold values from 0 to 7; in each aligned block of 128 rows (0 to 127, 128 to 255, ...) at most 24 rows name the same one
- losses: float32 [4096], P('dp'), may hold values from 1 to 30, as said below
- prior_weights: float32 [8], replicated, may hold values from 0.05 to 0.5
- norm_gain: float32 [4096], replicated, may hold values from 0.1 to 1.9
- gate_weight: bfloat16 [4096, 88064], P(None, ('dp', 'mp')), may hold values from -0.09375 to 0.09375
- up_weight: bfloat16 [4096, 88064], P(None, ('dp', 'mp')), may hold values from -0.09375 to 0.09375
- down_weight: bfloat16 [88064, 4096], P(('dp', 'mp')), may hold values from -0.25 to 0.25
Outputs:
- mixed: bfloat16 [4096, 4096], P('dp', 'mp')
- relative_weights: float32 [8], replicated
Inputs may be any that keep to these rules, and one draw needn't show every extreme that they name: `labels`: in each packed sequence no label is carried by more than 24 tokens, and in every draw some sequence has exactly 24 tokens of one label; every label occurs somewhere. `losses`: Positive.
All inputs are finite; a program needn't handle non-finite values.
Results may differ from a plain program's by a relative error of at most 0.014.
Values may be sent and summed in bfloat16 or wider, within the bound.
A program may use at most 128 MiB of HBM per device.

v0:
```python
import jax
import jax.numpy as jnp
from jax import lax
from jax.sharding import PartitionSpec as P

HEAD_DIM = 128
EXPERTS = 8
CAP = 24


dro_step = 0.5


def attend(queries, key_rows, value_rows, doc_lengths):
    seq_len = queries.shape[0]
    positions = jnp.arange(seq_len, dtype=jnp.int32)
    doc_ends = jnp.cumsum(doc_lengths)
    doc_ids = jnp.sum((positions[:, None] >= doc_ends[None, :]).astype(jnp.int32), axis=1)
    allowed = (doc_ids[:, None] == doc_ids[None, :]) & (positions[None, :] <= positions[:, None])
    q_heads = queries.reshape(seq_len, -1, HEAD_DIM)
    k_heads = key_rows.reshape(seq_len, -1, HEAD_DIM)
    v_heads = value_rows.reshape(seq_len, -1, HEAD_DIM)
    scores = jnp.einsum(
        "qhd,khd->hqk", q_heads, k_heads, preferred_element_type=jnp.float32
    ) * HEAD_DIM ** (-0.5)
    scores = jnp.where(allowed[None], scores, -1e30)
    row_max = jnp.max(scores, axis=-1, keepdims=True)
    exp_scores = jnp.exp(scores - row_max)
    attn_probs = (exp_scores / jnp.sum(exp_scores, axis=-1, keepdims=True)).astype(jnp.bfloat16)
    attn = jnp.einsum("hqk,khd->qhd", attn_probs, v_heads, preferred_element_type=jnp.float32)
    return attn.reshape(seq_len, -1)


def body(
    residual,
    queries,
    key_rows,
    value_rows,
    lengths,
    labels,
    losses,
    prior_weights,
    norm_gain,
    gate_weight,
    up_weight,
    down_weight,
):
    dp_count = lax.axis_size("dp")
    group_size = dp_count // EXPERTS
    tok_count = residual.shape[0]
    attn = attend(queries, key_rows, value_rows, lengths[0])
    hidden_state = (residual.astype(jnp.float32) + attn).astype(jnp.bfloat16)
    token_labels = labels[:, 0]
    expert_ids = jnp.arange(EXPERTS, dtype=jnp.int32)
    onehot_int = (token_labels[:, None] == expert_ids[None, :]).astype(jnp.int32)
    slot_rank = jnp.sum((jnp.cumsum(onehot_int, axis=0) - onehot_int) * onehot_int, axis=1)
    slot_ids = jnp.arange(CAP, dtype=jnp.int32)
    select = (
        (token_labels[None, None, :] == expert_ids[:, None, None])
        & (slot_rank[None, None, :] == slot_ids[None, :, None])
    ).astype(jnp.bfloat16)
    select = select.reshape(EXPERTS * CAP, tok_count)
    whole_rows = lax.all_gather(hidden_state, "mp", axis=1, tiled=True)
    packed = jnp.dot(select, whole_rows, preferred_element_type=jnp.float32).astype(jnp.bfloat16)
    arrived = lax.all_to_all(
        jnp.repeat(packed.reshape(EXPERTS, CAP, -1), group_size, axis=0),
        "dp",
        split_axis=0,
        concat_axis=0,
        tiled=True,
    )
    arrived_rows = arrived.reshape(dp_count * CAP, -1)
    rows_float = arrived_rows.astype(jnp.float32)
    scale_rows = lax.rsqrt(jnp.mean(rows_float * rows_float, axis=1, keepdims=True) + 1e-05)
    normed = (rows_float * scale_rows * norm_gain[None, :]).astype(jnp.bfloat16)
    gate_act = jnp.dot(normed, gate_weight, preferred_element_type=jnp.float32)
    up_act = jnp.dot(normed, up_weight, preferred_element_type=jnp.float32)
    inner_act = (jax.nn.silu(gate_act) * up_act).astype(jnp.bfloat16)
    partial_value = jnp.dot(inner_act, down_weight, preferred_element_type=jnp.float32)
    flat_slot = token_labels * CAP + slot_rank
    returned = lax.all_to_all(
        partial_value.reshape(dp_count, CAP, -1), "dp", split_axis=0, concat_axis=0, tiled=True
    )
    summed = jnp.sum(returned.reshape(EXPERTS, group_size, CAP, -1), axis=1).reshape(
        EXPERTS * CAP, -1
    )
    expert_out = lax.psum_scatter(
        summed[flat_slot].astype(jnp.bfloat16), "mp", scatter_dimension=1, tiled=True
    ).astype(jnp.float32)
    mixed = (hidden_state.astype(jnp.float32) + expert_out).astype(jnp.bfloat16)
    onehot = onehot_int.astype(jnp.float32)
    loss_total, token_count = lax.psum(
        (jnp.sum(onehot * losses[:, None], axis=0), jnp.sum(onehot, axis=0)), "dp"
    )
    domain_mean = loss_total / token_count
    scaled = prior_weights * jnp.exp(dro_step * domain_mean)
    relative_weights = EXPERTS * scaled / jnp.sum(scaled)
    return (mixed, relative_weights)


def solution(mesh):
    placed = (
        P("dp", "mp"),
        P("dp", "mp"),
        P("dp", "mp"),
        P("dp", "mp"),
        P("dp", None),
        P("dp", None),
        P("dp"),
        P(),
        P(),
        P(None, ("dp", "mp")),
        P(None, ("dp", "mp")),
        P(("dp", "mp"), None),
    )
    return jax.shard_map(
        body, mesh=mesh, in_specs=placed, out_specs=(P("dp", "mp"), P()), check_vma=False
    )
```

profile of v0, /device:TPU:1, one launch (start us, length us, event | category | flops | bytes accessed | tf_op | source)
XLA Modules:
  0.0 452.1 jit_solution(1040706692632113639)
XLA Ops:
  7.2 0.0 copy-start
  7.2 0.0 copy-start.5
  7.2 0.0 all-gather.2.cloned.1.call-start
  7.2 1.0 reduce-window.8
  8.2 0.1 convert_reduce_fusion.1
  8.3 0.1 fusion.23
  8.4 1.2 fusion.6
  9.6 0.1 fusion.28
  9.7 1.0 copy.30
  10.7 0.2 fusion.14
  10.9 0.1 copy.28
  11.1 1.6 add_convert_fusion.1
  12.6 0.0 all-gather.2.cloned.1.call-update
  12.7 0.0 copy-done.5
  12.7 0.1 fusion.22
  12.8 0.2 reduce_window_sum.18
  12.9 0.2 fusion.21
  13.2 37.0 %all-gather.2.cloned.1.call-done = bf16[128,4096]{1,0:T(8,128)(2,1)} async-done(((bf16[128,512]{1,0:T(8,128)(2,1)}), bf16[128,4096]{1,0:T(8,128)(2,1)}) %all-gather.2.cloned.1.call-update) | async-done | bytes 1048592 | tf_op jit(solution)/shard_map/all_gather | solution.py:63
  50.2 1.8 convolution_convert_fusion
  52.0 0.8 broadcast_in_dim.16
  52.8 85.6 %all_to_all.10 = bf16[32,24,4096]{2,1,0:T(8,128)(2,1)S(1)} all-to-all(bf16[32,24,4096]{2,1,0:T(8,128)(2,1)S(1)} %bitcast.51), channel_id=1, replica_groups=mesh['dp'=32,'mp'=8] {'dp'}, dimensions={0} | all-to-all | bytes 12582912 | tf_op jit(solution)/shard_map/all_to_all | solution.py:65
  138.4 0.0 copy-start.1
  138.4 0.0 copy-start.4
  138.4 1.3 multiply_reduce_fusion
  139.7 1.4 copy-done.1
  141.0 0.1 rsqrt.12
  141.1 0.0 copy-done.4
  141.1 0.0 copy-start.8
  141.1 5.5 %fusion.2 = bf16[768,4096]{1,0:T(8,128)(2,1)S(1)} fusion(f32[4096]{0:T(1024)S(1)} %copy-done.4, f32[768]{0:T(1024)S(1)} %rsqrt.12, bf16[32,24,4096]{2,1,0:T(8,128)(2,1)} %copy-done.1), kind=kLoop, calls=%fused_computation.5 | loop fusion | flops 12582912 | bytes 12602368 | tf_op jit(solution)/shard_map/convert_element_type | solution.py:75
  146.6 0.0 copy-start.2
  146.6 2.6 copy-done.2
  149.2 0.0 copy-done.8
  149.2 3.5 fusion.29
  152.7 0.0 copy-done
  152.7 15.9 %fusion.4 = f32[768,4096]{1,0:T(8,128)} fusion(bf16[344,4096]{1,0:T(8,128)(2,1)S(1)} %copy-done, bf16[768,4096]{1,0:T(8,128)(2,1)} %copy-done.2, bf16[4096,344]{0,1:T(8,128)(2,1)} %param.22, f32[768,344]{0,1:T(8,128)} %fusion.29), kind=kOutput, calls=%fused_computation.10 | convolution fusion | flops 4330106880 | bytes 25567232 | tf_op jit(solution)/shard_map/dot_general | solution.py:79
  168.6 4.9 %all-to-all-start.1 = ((f32[32,24,4096]{2,1,0:T(8,128)}), f32[32,24,4096]{2,1,0:T(8,128)}, u32[]{:S(2)}, u32[]{:S(2)}) async-start(f32[32,24,4096]{2,1,0:T(8,128)} %bitcast.52), calls=%async_computation.1 | async-start | bytes 25165824 | tf_op jit(solution)/shard_map/all_to_all | solution.py:81
  173.5 0.0 reduce-scatter.2.cloned.1.call-start
  173.6 173.7 %all-to-all-done.1 = f32[32,24,4096]{2,1,0:T(8,128)} async-done(((f32[32,24,4096]{2,1,0:T(8,128)}), f32[32,24,4096]{2,1,0:T(8,128)}, u32[]{:S(2)}, u32[]{:S(2)}) %all-to-all-start.1) | async-done | bytes 12582944 | tf_op jit(solution)/shard_map/all_to_all | solution.py:81
  347.2 7.4 %bitcast_reduce_fusion = bf16[8,24,4096]{2,1,0:T(8,128)(2,1)} fusion(f32[32,24,4096]{2,1,0:T(8,128)} %all-to-all-done.1), kind=kLoop, calls=%fused_computation.2 | loop fusion | flops 2359296 | bytes 14155776 | tf_op jit(solution)/shard_map/reduce_sum | solution.py:84
  354.6 0.0 copy-start.7
  354.6 0.0 copy-start.6
  354.6 0.0 copy-start.3
  354.6 4.8 %gather_fusion = bf16[128,4096]{1,0:T(8,128)(2,1)} fusion(bf16[192,4096]{1,0:T(8,128)(2,1)} %bitcast.50, s32[1024]{0:T(1024)S(1)} %pad_clamp_fusion), kind=kCustom, calls=%fused_computation | custom fusion | bytes 2097664 | tf_op jit(solution)/shard_map/gather | solution.py:88
  359.4 0.0 reduce-scatter.2.cloned.1.call-update
  359.5 0.0 copy-done.7
  359.5 0.1 convert_reduce_fusion
  359.6 82.4 %all-reduce = (f32[8]{0:T(128)S(1)}, f32[8]{0:T(128)S(1)}) all-reduce(f32[8]{0:T(128)S(1)} %get-tuple-element.3, f32[8]{0:T(128)S(1)} %get-tuple-element.2), channel_id=1, replica_groups=mesh['dp'=32,'mp'=8] {'dp'}, use_global_device_ids=true, to_apply=%region_10.11 | all-reduce | flops 16 | bytes 128 | tf_op jit(solution)/shard_map/psum | solution.py:92
  442.0 0.0 copy-done.6
  442.0 0.6 fusion.27
  442.6 1.1 multiply_divide_fusion
  443.7 0.0 reduce-scatter.2.cloned.1.call-done
  443.7 0.0 copy-done.3
  443.7 1.6 add_convert_fusion
  (6 shorter events, 0.1 us)
Async XLA Ops:
  7.2 145.5 %copy-start = (bf16[344,4096]{1,0:T(8,128)(2,1)S(1)}, bf16[344,4096]{1,0:T(8,128)(2,1)}, u32[]{:S(2)}) copy-start(bf16[344,4096]{1,0:T(8,128)(2,1)} %param.23) | copy-start | bytes 8454148
  7.2 5.5 %copy-start.5 = (s32[128,1]{0,1:T(1,128)S(1)}, s32[128,1]{0,1:T(1,128)}, u32[]{:S(2)}) copy-start(s32[128,1]{0,1:T(1,128)} %param.17) | copy-start | bytes 1540
  7.2 43.0 %all-gather.2.cloned.1.call-start = ((), (), s32[]{:S(2)}) async-start(), calls=%async_computation.3 | async-start | bytes 1179648 | tf_op jit(solution)/shard_map/all_gather | solution.py:63
  138.4 2.7 copy-start.1
  138.4 2.8 copy-start.4
  141.1 8.1 %copy-start.8 = (bf16[4096,344]{0,1:T(8,128)(2,1)S(1)}, bf16[4096,344]{0,1:T(8,128)(2,1)}, u32[]{:S(2)}) copy-start(bf16[4096,344]{0,1:T(8,128)(2,1)} %param.21) | copy-start | bytes 8454148
  146.6 2.6 copy-start.2
  168.6 178.6 %all-to-all-start.1 = ((f32[32,24,4096]{2,1,0:T(8,128)}), f32[32,24,4096]{2,1,0:T(8,128)}, u32[]{:S(2)}, u32[]{:S(2)}) async-start(f32[32,24,4096]{2,1,0:T(8,128)} %bitcast.52), calls=%async_computation.1 | async-start | bytes 25165824 | tf_op jit(solution)/shard_map/all_to_all | solution.py:81
  173.5 270.2 %reduce-scatter.2.cloned.1.call-start = ((), (), s32[]{:S(2)}) async-start(), calls=%async_computation.4 | async-start | bytes 1179648 | tf_op jit(solution)/shard_map/reduce_scatter | solution.py:87
  354.6 4.8 %copy-start.7 = (f32[128]{0:T(128)S(1)}, f32[128]{0:T(128)}, u32[]{:S(2)}) copy-start(f32[128]{0:T(128)} %param.18) | copy-start | bytes 1540
  354.6 87.4 %copy-start.6 = (f32[8]{0:T(128)S(1)}, f32[8]{0:T(128)}, u32[]{:S(2)}) copy-start(f32[8]{0:T(128)} %param.19) | copy-start | bytes 100
  354.6 89.1 %copy-start.3 = (bf16[128,512]{1,0:T(8,128)(2,1)S(1)}, bf16[128,512]{1,0:T(8,128)(2,1)}, u32[]{:S(2)}) copy-start(bf16[128,512]{1,0:T(8,128)(2,1)} %add_convert_fusion.1) | copy-start | bytes 393220
Sparse Core Ops, SparseCore 0:
  12.8 37.3 all-gather.1
  359.6 55.7 reduce-scatter.1
where the time goes:
time: 453 us; the launch traced here: 452 us
  waiting for transfers between devices  211 us (47%)
  blocking collectives  168 us (37%)
  matrix products  22.5 us (5%)
  other arithmetic  20.8 us (5%)
  between operations  14.2 us (3%)
  local copies, waits for them, and re-layouts  10.8 us (2%)
  starting transfers between devices  4.95 us (1%)
    all_to_all x1, waiting for transfers between devices, body(): lax.all_to_all(partial_value.reshape(dp_count, CAP, -1), 'dp', split_axis...  174 us
    all_to_all x1, blocking collectives, body(): lax.all_to_all(jnp.repeat(packed.reshape(EXPERTS, CAP, -1), group_size, a...  85.6 us
    psum x1, blocking collectives, body(): lax.psum((jnp.sum(onehot * losses[:, None], axis=0), jnp.sum(onehot, axis...  82.4 us
    all_gather x1, waiting for transfers between devices, body(): whole_rows = lax.all_gather(hidden_state, 'mp', axis=1, tiled=True)  37 us
    dot_general x1, matrix products, body(): jnp.dot(inner_act, down_weight, preferred_element_type=jnp.float32)  15.9 us
  transfers between devices with their start and end apart: 3, of which 2 were waited for; matrix products, arithmetic and copies ran while one was open for 1% of the time, Pallas kernels for 0%

commit v1 on v0

v1 whole, which is shorter than its diff:
```python
import jax
import jax.numpy as jnp
from jax import lax
from jax.experimental import pallas as pl
from jax.experimental.pallas import tpu as pltpu
from jax.sharding import PartitionSpec as P

HEAD_DIM = 128
EXPERTS = 8
CAP = 24
PAD = 32
TOK = 128
COLS = 512
HID = 344
NZ = 8
CORE_ROWS = 16 * CAP
ROWS = 2 * CORE_ROWS
CHUNK = 4 * CAP
SHARED = 2 * CHUNK
RIGHT, LEFT = 0, 1
F32, BF16 = jnp.float32, jnp.bfloat16
MESH = pl.DeviceIdType.MESH

dro_step = 0.5


def kernel(
    lengths_ref, labels_ref, losses_ref, prior_ref, gain_ref,
    res_hbm, q_hbm, k_hbm, v_hbm, gate_hbm, up_hbm, down_hbm,
    mixed_ref, weights_ref,
    res_v, q_v, k_v, v_v, gate_v, up_v, down_v,
    hidden, packed, stage, xb, acc_g, acc_u, square, inner,
    part, sib_out, sib_in, ring_in, ring_out, y_out, y_in, ret_out, ret,
    stat_x, stat_y, stat_c, stat_src,
    in_sem, w_sem, a_send, a_recv, g_send, g_recv, gs_send, gs_recv, gy_send, gy_recv,
    rs_send, rs_recv, ry_send, ry_recv, r_send, r_recv, b_send, b_recv, st_send, st_recv,
):
    dp = lax.axis_index("dp")
    z = lax.axis_index("mp")
    core = lax.rem(dp, 2)
    xy = dp // 2
    x, y = xy // 4, lax.rem(xy, 4)
    yb = lax.rem(y, 2)

    def plane(tx, ty, tc=None):
        return ((tx * 4 + ty) * 2 + (core if tc is None else tc), z)

    sibling = (dp + 1 - 2 * core, z)
    partner = plane(x, y + 1 - 2 * yb)
    z_right = (dp, lax.rem(z + 1, NZ))
    z_left = (dp, lax.rem(z + NZ - 1, NZ))
    toward = (z_right, z_left)
    offsets = [((i // 4), i % 4) for i in range(1, 16)]

    barrier = pltpu.get_barrier_semaphore()
    peers = [plane(lax.rem(x + dx, 4), lax.rem(y + dy, 4)) for dx, dy in offsets]
    peers += [sibling, z_right, z_left]
    for peer in peers:
        pl.semaphore_signal(barrier, inc=1, device_id=peer, device_id_type=MESH)

    loads = [
        pltpu.make_async_copy(src, dst, in_sem.at[i])
        for i, (src, dst) in enumerate(((q_hbm, q_v), (k_hbm, k_v), (v_hbm, v_v), (res_hbm, res_v)))
    ]
    for load in loads:
        load.start()
    weight_loads = [
        pltpu.make_async_copy(gate_hbm, gate_v, w_sem.at[0]),
        pltpu.make_async_copy(up_hbm, up_v, w_sem.at[1]),
    ] + [
        pltpu.make_async_copy(down_hbm.at[:, pl.ds(i * COLS, COLS)], down_v.at[i], w_sem.at[2 + i])
        for i in range(NZ)
    ]
    for load in weight_loads:
        load.start()

    def remote(src, dst, send, recv, device):
        return pltpu.make_async_remote_copy(
            src_ref=src, dst_ref=dst, send_sem=send, recv_sem=recv,
            device_id=device, device_id_type=MESH,
        )

    at0 = lax.broadcasted_iota(jnp.int32, (TOK, TOK), 0)
    at1 = lax.broadcasted_iota(jnp.int32, (TOK, TOK), 1)
    label_col = labels_ref[...].astype(F32)
    label_row = jnp.sum(jnp.where(at0 == at1, label_col, 0.0), axis=0, keepdims=True)
    same = label_col == label_row
    rank_row = jnp.sum(jnp.where(same & (at0 < at1), 1.0, 0.0), axis=0, keepdims=True)
    rank_col = jnp.sum(jnp.where(same & (at1 < at0), 1.0, 0.0), axis=1, keepdims=True)
    slot_row = label_row * PAD + rank_row
    slot_ids = lax.broadcasted_iota(jnp.int32, (EXPERTS * PAD, TOK), 0).astype(F32)
    select = (slot_ids == slot_row).astype(BF16)

    domain = lax.broadcasted_iota(jnp.int32, (EXPERTS, TOK), 0).astype(F32)
    lane = lax.broadcasted_iota(jnp.int32, (EXPERTS, TOK), 1)
    member = (domain == label_row).astype(F32)
    loss_sum = jnp.sum(member * losses_ref[...], axis=1, keepdims=True)
    count = jnp.sum(member, axis=1, keepdims=True)
    stat_src[0] = jnp.where(lane == 0, loss_sum, jnp.where(lane == 1, count, 0.0))

    ends = [lengths_ref[0, 0]]
    for i in range(1, 4):
        ends.append(ends[-1] + lengths_ref[0, i])
    doc0 = sum((at0 >= end).astype(jnp.int32) for end in ends)
    doc1 = sum((at1 >= end).astype(jnp.int32) for end in ends)
    allowed = (doc0 == doc1) & (at1 <= at0)
    for load in loads:
        load.wait()
    for head in range(COLS // HEAD_DIM):
        cut = slice(head * HEAD_DIM, (head + 1) * HEAD_DIM)
        scores = lax.dot_general(
            q_v[:, cut], k_v[:, cut], (((1,), (1,)), ((), ())), preferred_element_type=F32
        ) * HEAD_DIM ** (-0.5)
        scores = jnp.where(allowed, scores, -1e30)
        exp_scores = jnp.exp(scores - jnp.max(scores, axis=1, keepdims=True))
        probs = (exp_scores / jnp.sum(exp_scores, axis=1, keepdims=True)).astype(BF16)
        attn = jnp.dot(probs, v_v[:, cut], preferred_element_type=F32)
        hidden[:, cut] = (res_v[:, cut].astype(F32) + attn).astype(BF16)
    packed[...] = (
        jnp.dot(select, hidden[...], preferred_element_type=F32)
        .astype(BF16)
        .reshape(EXPERTS, PAD, COLS)
    )

    pl.semaphore_wait(barrier, len(peers))

    my_q = jnp.where(x >= 2, (x - 2) * 4 + y, 8 + y)

    def goes(ty):
        return (x >= 2) | (lax.rem(ty, 2) == x)

    def send_block(i):
        dx, dy = offsets[i]
        tx, ty = lax.rem(x + dx, 4), lax.rem(y + dy, 4)
        copy = remote(
            packed.at[2 * tx + ty // 2], stage.at[my_q], a_send.at[i], a_recv.at[my_q], plane(tx, ty)
        )
        return goes(ty), copy

    for i in range(15):
        allowed_i, copy = send_block(i)
        pl.when(allowed_i)(copy.start)

    @pl.when(goes(y))
    def _():
        stage[my_q] = packed[2 * x + y // 2]

    def seq_of(q):
        if q < 8:
            return 2 + q // 4, q % 4
        return yb, q - 8

    def stat_copy(i, phase):
        if phase == 0:
            dst, peer = stat_x, plane(lax.rem(x + i, 4), y)
            return remote(stat_src.at[0], dst.at[x], st_send.at[i - 1], st_recv.at[x], peer)
        if phase == 1:
            dst, peer = stat_y, plane(x, lax.rem(y + i, 4))
            return remote(stat_src.at[1], dst.at[y], st_send.at[2 + i], st_recv.at[4 + y], peer)
        return remote(stat_src.at[2], stat_c, st_send.at[6], st_recv.at[8], sibling)

    def stat_wait(i, phase):
        if phase == 0:
            at = lax.rem(x + i, 4)
            return remote(stat_src.at[0], stat_x.at[at], st_send.at[0], st_recv.at[at], plane(at, y))
        at = lax.rem(y + i, 4)
        return remote(stat_src.at[1], stat_y.at[at], st_send.at[0], st_recv.at[4 + at], plane(x, at))

    for i in range(1, 4):
        stat_copy(i, 0).start()
    stat_x[x] = stat_src[0]

    base = core * CORE_ROWS
    sib_base = (1 - core) * CORE_ROWS
    own_off = SHARED + yb * CHUNK
    other_off = SHARED + (1 - yb) * CHUNK
    OWN, C0, C1, OTHER = 0, 1, 2, 3
    piece_off = (own_off, 0, CHUNK, other_off)

    def slice_at(rel):
        return lax.rem(z + rel, NZ)

    def block(rel, off, rows):
        start = pl.multiple_of(base + off, 16)
        return xb.at[slice_at(rel), pl.ds(start, rows)]

    def gather_copy(way, hop, piece, sending, off=None, rows=CHUNK):
        sign = 1 if way == LEFT else -1
        behind = hop - 1 if sending else hop
        rel = (sign * behind) % NZ
        ref = block(rel, piece_off[piece] if off is None else off, rows)
        return remote(
            ref, ref, g_send.at[way, hop - 1, piece], g_recv.at[way, hop - 1, piece], toward[way]
        )

    HALF = CHUNK // 2
    far = {
        (RIGHT, OWN): dict(off=own_off, rows=CHUNK),
        (RIGHT, C0): dict(off=0, rows=HALF),
        (LEFT, C0): dict(off=HALF, rows=HALF),
        (LEFT, C1): dict(off=CHUNK, rows=CHUNK),
    }

    def sib_copy(rel, piece, mine=True):
        start = pl.multiple_of((base if mine else sib_base) + piece_off[piece], 16)
        ref = xb.at[slice_at(rel), pl.ds(start, CHUNK)]
        return remote(ref, ref, gs_send.at[rel, piece], gs_recv.at[rel, piece], sibling)

    def y_copy(rel, mine=True):
        ref = block(rel, own_off if mine else other_off, CHUNK)
        return remote(ref, ref, gy_send.at[rel], gy_recv.at[rel], partner)

    started = []

    def go(copy):
        copy.start()
        started.append(copy)

    def spread(rel, piece):
        if piece == OWN:
            go(y_copy(rel))
        go(sib_copy(rel, piece))

    for piece, first in ((OWN, 8), (C0, 0), (C1, 4)):
        for q in range(first, first + 4):
            sx, sy = seq_of(q)
            arrival = remote(
                packed.at[0], stage.at[q], a_send.at[0], a_recv.at[q], plane(sx, sy)
            )
            pl.when((sx != x) | (sy != y))(arrival.wait_recv)
        rows = stage[first:first + 4].astype(F32)[:, :CAP].reshape(CHUNK, COLS).astype(BF16)
        start = pl.multiple_of(base + piece_off[piece], 16)
        xb[z, pl.ds(start, CHUNK)] = rows
        go(gather_copy(RIGHT, 1, piece, True))
        go(gather_copy(LEFT, 1, piece, True))
        spread(0, piece)

    for ref in (acc_g, acc_u, square):
        ref[...] = jnp.zeros_like(ref)

    BLOCK = SHARED

    def multiply(rels, rows_from):
        def one(i, carry):
            rel = rels[0] if len(rels) == 1 else jnp.where(i == 0, rels[0], rels[1])
            s = slice_at(rel)
            at = pl.multiple_of(s * COLS, COLS)
            gain = gain_ref[pl.ds(s, 1), :]
            for start in rows_from:
                here = pl.ds(pl.multiple_of(start, 16), BLOCK)
                value = xb[s, here, :].astype(F32)
                sq = value * value
                square[here, :] += (
                    sq[:, :128] + sq[:, 128:256] + sq[:, 256:384] + sq[:, 384:]
                )
                scaled = (value * gain).astype(BF16)
                acc_g[here, :] += jnp.dot(
                    scaled, gate_v[pl.ds(at, COLS), :], preferred_element_type=F32
                )
                acc_u[here, :] += jnp.dot(
                    scaled, up_v[pl.ds(at, COLS), :], preferred_element_type=F32
                )
            return carry

        lax.fori_loop(0, len(rels), one, 0)

    def settle(rels, j):
        if j == 0:
            for rel in rels:
                y_copy(rel, mine=False).wait_recv()
                go(sib_copy(rel, OTHER))
            multiply(rels, (base,))
        elif j == 1:
            for rel in rels:
                sib_copy(rel, C0, mine=False).wait_recv()
                sib_copy(rel, C1, mine=False).wait_recv()
            multiply(rels, (sib_base,))
        else:
            for rel in rels:
                sib_copy(rel, OWN, mine=False).wait_recv()
                sib_copy(rel, OTHER, mine=False).wait_recv()
            multiply(rels, (base + SHARED, sib_base + SHARED))

    weight_loads[0].wait()
    weight_loads[1].wait()
    before = (0,)
    for hop in (1, 2, 3):
        for j, piece in enumerate((OWN, C0, C1)):
            for way in (RIGHT, LEFT):
                gather_copy(way, hop, piece, False).wait_recv()
                if hop < 3:
                    go(gather_copy(way, hop + 1, piece, True))
                elif (way, piece) in far:
                    go(gather_copy(way, 4, piece, True, **far[way, piece]))
                spread(hop if way == LEFT else NZ - hop, piece)
            settle(before, j)
        before = (hop, NZ - hop)
        if hop == 1:
            for i in range(1, 4):
                stat_wait(i, 0).wait_recv()
            stat_src[1] = (stat_x[0] + stat_x[1]) + (stat_x[2] + stat_x[3])
            for i in range(1, 4):
                stat_copy(i, 1).start()
            stat_y[y] = stat_src[1]
        if hop == 2:
            for i in range(1, 4):
                stat_wait(i, 1).wait_recv()
            stat_src[2] = (stat_y[0] + stat_y[1]) + (stat_y[2] + stat_y[3])
            stat_copy(0, 2).start()
    gather_copy(RIGHT, 4, OWN, False, **far[RIGHT, OWN]).wait_recv()
    spread(4, OWN)
    settle(before, 0)
    gather_copy(RIGHT, 4, C0, False, **far[RIGHT, C0]).wait_recv()
    gather_copy(LEFT, 4, C0, False, **far[LEFT, C0]).wait_recv()
    spread(4, C0)
    settle(before, 1)
    gather_copy(LEFT, 4, C1, False, **far[LEFT, C1]).wait_recv()
    spread(4, C1)
    settle(before, 2)
    for j in range(3):
        settle((4,), j)

    def activate(i, carry):
        here = pl.ds(pl.multiple_of(i * BLOCK, BLOCK), BLOCK)
        mean = jnp.sum(square[here, :], axis=1, keepdims=True) * (1.0 / (NZ * COLS))
        scale = lax.rsqrt(mean + 1e-05)
        gate = acc_g[here, :] * scale
        up = acc_u[here, :] * scale
        inner[here, :] = (gate / (1.0 + jnp.exp(-gate)) * up).astype(BF16)
        return carry

    lax.fori_loop(0, ROWS // BLOCK, activate, 0)
    for load in weight_loads[2:]:
        load.wait()

    def rs_copy(rel):
        return remote(
            sib_out.at[rel], sib_in.at[rel], rs_send.at[rel], rs_recv.at[rel], sibling
        )

    def ry_copy(rel):
        return remote(y_out.at[rel], y_in.at[rel], ry_send.at[rel], ry_recv.at[rel], partner)

    def prepare(rel):
        weight = down_v.at[slice_at(rel)]

        def one(i, carry):
            off = pl.multiple_of(i * BLOCK, BLOCK)
            theirs = inner[pl.ds(pl.multiple_of(sib_base + off, 16), BLOCK), :]
            sib_out[rel, pl.ds(off, BLOCK)] = jnp.dot(
                theirs, weight[...], preferred_element_type=F32
            ).astype(BF16)
            return carry

        lax.fori_loop(0, 2, one, 0)
        go(rs_copy(rel))

        def two(i, carry):
            off = pl.multiple_of(i * BLOCK, BLOCK)
            mine = inner[pl.ds(pl.multiple_of(base + off, 16), BLOCK), :]
            part[rel, pl.ds(off, BLOCK)] = jnp.dot(mine, weight[...], preferred_element_type=F32)
            return carry

        lax.fori_loop(0, 2, two, 0)

    def join(rel):
        rs_copy(rel).wait_recv()
        other = pl.ds(pl.multiple_of(other_off, 16), CHUNK)
        y_out[rel] = (part[rel, other] + sib_in[rel, other].astype(F32)).astype(BF16)
        go(ry_copy(rel))
        own = pl.ds(pl.multiple_of(own_off, 16), CHUNK)
        part[rel, own] += sib_in[rel, own].astype(F32)
        part[rel, :SHARED] += sib_in[rel, :SHARED].astype(F32)

    def ring_copy(way, left_to_go, piece, off, rows):
        here = pl.ds(pl.multiple_of(off, 16), rows)
        return remote(
            ring_out.at[way, left_to_go - 1, here],
            ring_in.at[way, left_to_go - 1, here],
            r_send.at[way, left_to_go - 1, piece],
            r_recv.at[way, left_to_go - 1, piece],
            toward[way],
        )

    def rel_of(way, distance):
        return distance if way == RIGHT else (NZ - distance) % NZ

    def own_sum(rel, piece, off, rows):
        value = part[rel, pl.ds(pl.multiple_of(off, 16), rows)]
        if piece == OWN:
            value = value + y_in[rel].astype(F32)
        return value

    def emit(way, distance, piece, off, rows, value):
        here = pl.ds(pl.multiple_of(off, 16), rows)
        ring_out[way, distance - 1, here] = value.astype(BF16)
        go(ring_copy(way, distance, piece, off, rows))

    def incoming(way, distance, piece, off, rows):
        ring_copy(way, distance, piece, off, rows).wait_recv()
        return ring_in[way, distance - 1, pl.ds(pl.multiple_of(off, 16), rows)].astype(F32)

    gather_started = list(started)
    started.clear()
    prepare(4)
    prepare(3)
    join(4)
    for way, piece in ((RIGHT, C0), (LEFT, C0), (LEFT, C1)):
        spec = far[way, piece]
        emit(way, 4, piece, spec["off"], spec["rows"], own_sum(4, piece, **spec))
    prepare(5)
    join(3)
    ry_copy(4).wait_recv()
    spec = far[RIGHT, OWN]
    emit(RIGHT, 4, OWN, spec["off"], spec["rows"], own_sum(4, OWN, **spec))
    join(5)
    prepare(2)
    prepare(6)
    pieces = ((C0, 0), (C1, CHUNK), (OWN, own_off))
    for distance in (3, 2, 1):
        for piece, off in pieces:
            for way in (RIGHT, LEFT):
                rel = rel_of(way, distance)
                if piece == OWN:
                    ry_copy(rel).wait_recv()
                value = own_sum(rel, piece, off, CHUNK)
                if distance < 3:
                    value = value + incoming(way, distance + 1, piece, off, CHUNK)
                    emit(way, distance, piece, off, CHUNK, value)
                elif (way, piece) in far:
                    spec = far[way, piece]
                    arrived = incoming(way, 4, piece, spec["off"], spec["rows"])
                    if spec["rows"] == CHUNK:
                        value = value + arrived
                    elif way == RIGHT:
                        value = jnp.concatenate([value[:HALF] + arrived, value[HALF:]], axis=0)
                    else:
                        value = jnp.concatenate([value[:HALF], value[HALF:] + arrived], axis=0)
                    emit(way, distance, piece, off, CHUNK, value)
                else:
                    emit(way, distance, piece, off, CHUNK, value)
        if distance > 1:
            join(distance - 1)
            join(NZ - distance + 1)
            if distance == 3:
                prepare(1)
                prepare(7)
            else:
                prepare(0)
        else:
            join(0)
            for copy in gather_started:
                copy.wait_send()

    def send_back(q):
        sx, sy = seq_of(q)
        return remote(ret_out.at[q], ret.at[xy], b_send.at[q], b_recv.at[xy], plane(sx, sy))

    def is_me(q):
        sx, sy = seq_of(q)
        return (sx == x) & (sy == y)

    for piece, off in pieces:
        if piece == OWN:
            ry_copy(0).wait_recv()
        value = own_sum(0, piece, off, CHUNK)
        value = value + incoming(RIGHT, 1, piece, off, CHUNK)
        value = value + incoming(LEFT, 1, piece, off, CHUNK)
        first = {C0: 0, C1: 4, OWN: 8}[piece]
        value = jnp.concatenate(
            [value.reshape(4, CAP, COLS), jnp.zeros((4, PAD - CAP, COLS), F32)], axis=1
        )
        ret_out[first:first + 4] = value.astype(BF16)
        for q in range(first, first + 4):
            pl.when(jnp.logical_not(is_me(q)))(send_back(q).start)

    @pl.when(goes(y))
    def _():
        ret[xy] = ret_out[my_q]

    for i in range(16):
        @pl.when(jnp.logical_not(goes(i % 4)))
        def _():
            ret[i] = jnp.zeros((PAD, COLS), BF16)

    stat_copy(0, 2).wait_recv()
    totals = stat_src[2] + stat_c[...]
    domain_mean = totals[:, 0:1] / totals[:, 1:2]
    eye = lax.broadcasted_iota(jnp.int32, (EXPERTS, EXPERTS), 0) == lax.broadcasted_iota(
        jnp.int32, (EXPERTS, EXPERTS), 1
    )
    mean_row = jnp.sum(jnp.where(eye, domain_mean, 0.0), axis=0, keepdims=True)
    scaled = prior_ref[...] * jnp.exp(dro_step * mean_row)
    weights_ref[...] = EXPERTS * scaled / jnp.sum(scaled, axis=1, keepdims=True)

    for copy in started:
        copy.wait_send()
    for i in range(15):
        allowed_i, copy = send_block(i)
        pl.when(allowed_i)(copy.wait_send)
    for i in range(1, 4):
        stat_copy(i, 0).wait_send()
        stat_copy(i, 1).wait_send()
    stat_copy(0, 2).wait_send()

    place = lax.broadcasted_iota(jnp.int32, (TOK, 16 * PAD), 1).astype(F32)
    spot = label_col * (2 * PAD) + rank_col
    take = ((place == spot) | (place == spot + PAD)).astype(BF16)
    for i in range(16):
        arrival = remote(
            ret_out.at[0], ret.at[i], b_send.at[0], b_recv.at[i], plane(i // 4, i % 4)
        )
        pl.when(goes(i % 4) & (xy != i))(arrival.wait_recv)
    expert_out = jnp.dot(take, ret[...].reshape(16 * PAD, COLS), preferred_element_type=F32)
    mixed_ref[...] = (hidden[...].astype(F32) + expert_out).astype(BF16)
    for q in range(12):
        pl.when(jnp.logical_not(is_me(q)))(send_back(q).wait_send)


def body(
    residual, queries, key_rows, value_rows, lengths, labels, losses, prior_weights, norm_gain,
    gate_weight, up_weight, down_weight,
):
    vmem = pl.BlockSpec(memory_space=pltpu.VMEM)
    smem = pl.BlockSpec(memory_space=pltpu.SMEM)
    hbm = pl.BlockSpec(memory_space=pl.ANY)
    dma = pltpu.SemaphoreType.DMA
    tile = (TOK, COLS)
    mixed, weights = pl.pallas_call(
        kernel,
        out_shape=(
            jax.ShapeDtypeStruct(tile, BF16),
            jax.ShapeDtypeStruct((1, EXPERTS), F32),
        ),
        in_specs=[smem, vmem, vmem, vmem, vmem] + [hbm] * 7,
        out_specs=(vmem, vmem),
        scratch_shapes=[
            pltpu.VMEM(tile, BF16),
            pltpu.VMEM(tile, BF16),
            pltpu.VMEM(tile, BF16),
            pltpu.VMEM(tile, BF16),
            pltpu.VMEM((NZ * COLS, HID), BF16),
            pltpu.VMEM((NZ * COLS, HID), BF16),
            pltpu.VMEM((NZ, HID, COLS), BF16),
            pltpu.VMEM(tile, BF16),
            pltpu.VMEM((EXPERTS, PAD, COLS), BF16),
            pltpu.VMEM((12, PAD, COLS), BF16),
            pltpu.VMEM((NZ, ROWS, COLS), BF16),
            pltpu.VMEM((ROWS, HID), F32),
            pltpu.VMEM((ROWS, HID), F32),
            pltpu.VMEM((ROWS, 128), F32),
            pltpu.VMEM((ROWS, HID), BF16),
            pltpu.VMEM((NZ, CORE_ROWS, COLS), F32),
            pltpu.VMEM((NZ, CORE_ROWS, COLS), BF16),
            pltpu.VMEM((NZ, CORE_ROWS, COLS), BF16),
            pltpu.VMEM((2, 4, CORE_ROWS, COLS), BF16),
            pltpu.VMEM((2, 4, CORE_ROWS, COLS), BF16),
            pltpu.VMEM((NZ, CHUNK, COLS), BF16),
            pltpu.VMEM((NZ, CHUNK, COLS), BF16),
            pltpu.VMEM((12, PAD, COLS), BF16),
            pltpu.VMEM((16, PAD, COLS), BF16),
            pltpu.VMEM((4, EXPERTS, 128), F32),
            pltpu.VMEM((4, EXPERTS, 128), F32),
            pltpu.VMEM((EXPERTS, 128), F32),
            pltpu.VMEM((3, EXPERTS, 128), F32),
            dma((4,)), dma((2 + NZ,)),
            dma((15,)), dma((12,)),
            dma((2, 4, 3)), dma((2, 4, 3)),
            dma((NZ, 4)), dma((NZ, 4)),
            dma((NZ,)), dma((NZ,)),
            dma((NZ,)), dma((NZ,)),
            dma((NZ,)), dma((NZ,)),
            dma((2, 4, 3)), dma((2, 4, 3)),
            dma((12,)), dma((16,)),
            dma((7,)), dma((9,)),
        ],
        compiler_params=pltpu.CompilerParams(
            collective_id=0, has_side_effects=True, vmem_limit_bytes=60 * 1024 * 1024
        ),
    )(
        lengths, labels, losses.reshape(1, TOK), prior_weights.reshape(1, EXPERTS),
        norm_gain.reshape(NZ, COLS), residual, queries, key_rows, value_rows,
        gate_weight, up_weight, down_weight,
    )
    return (mixed, weights.reshape(EXPERTS))


def solution(mesh):
    placed = (
        P("dp", "mp"),
        P("dp", "mp"),
        P("dp", "mp"),
        P("dp", "mp"),
        P("dp", None),
        P("dp", None),
        P("dp"),
        P(),
        P(),
        P(None, ("dp", "mp")),
        P(None, ("dp", "mp")),
        P(("dp", "mp"), None),
    )
    return jax.shard_map(
        body, mesh=mesh, in_specs=placed, out_specs=(P("dp", "mp"), P()), check_vma=False
    )
```

time: 453 us -> 102 us (0.23)
  waiting for transfers between devices: 211 us -> 0 us
  blocking collectives: 168 us -> 0 us
  Pallas kernels: 0 us -> 87.9 us
  matrix products: 22.5 us -> 0 us
  other arithmetic: 20.8 us -> 0 us
  between operations: 14.2 us -> 0.64 us
  starting transfers between devices: 4.95 us -> 0 us
    all_to_all x1 -> x0, waiting for transfers between devices: 174 us -> none  [body(): lax.all_to_all(partial_value.reshape(dp_count, CAP, -1), 'dp', split_axis...]
    pallas_call x0 -> x1, Pallas kernels: none -> 87.9 us  [body(): pl.pallas_call(kernel, out_shape=(jax.ShapeDtypeStruct(tile, BF16), jax.S...]
    all_to_all x1 -> x0, blocking collectives: 85.6 us -> none  [body(): lax.all_to_all(jnp.repeat(packed.reshape(EXPERTS, CAP, -1), group_size, a...]
    psum x1 -> x0, blocking collectives: 82.4 us -> none  [body(): lax.psum((jnp.sum(onehot * losses[:, None], axis=0), jnp.sum(onehot, axis...]
    all_gather x1 -> x0, waiting for transfers between devices: 37 us -> none  [body(): whole_rows = lax.all_gather(hidden_state, 'mp', axis=1, tiled=True)]
    dot_general x5 -> x0, matrix products: 22.5 us -> none  [the longest x1 15.9 us: body(): jnp.dot(inner_act, down_weight, preferred_element_type=jnp.float32)]
    reduce_sum x6 -> x0, other arithmetic: 9.64 us -> none  [the longest x1 7.36 us: body(): jnp.sum(returned.reshape(EXPERTS, group_size, CAP, -1), axis=1)]
    convert_element_type x4 -> x0, other arithmetic: 8.73 us -> none  [the longest x1 5.47 us: body(): normed = (rows_float * scale_rows * norm_gain[None, :]).astype(jnp.bfloat16)]
  transfers between devices with their start and end apart: 3 -> 0, of which waited for: 2 -> 0; matrix products, arithmetic and copies ran while one was open for 1% -> 0% of each run, Pallas kernels for 0% -> 0%
where the time goes in v1:
time: 102 us; the launch traced here: 101 us
  Pallas kernels  87.9 us (86%)
  local copies, waits for them, and re-layouts  12.9 us (13%)
    pallas_call x1, Pallas kernels, body(): pl.pallas_call(kernel, out_shape=(jax.ShapeDtypeStruct(tile, BF16), jax.S...  87.9 us
    unnamed x7, local copies, waits for them, and re-layouts  11.6 us

profile of v1, /device:TPU:1, one launch (start us, length us, event | category | flops | bytes accessed | tf_op | source)
XLA Modules:
  0.0 101.4 jit_solution(14351659628540460746)
XLA Ops:
  0.6 1.3 %reshape.18.gain_ref = f32[8,512]{1,0:T(8,128)} reshape(f32[4096]{0:T(1024)} %param.20) | data formatting | bytes 32768 | tf_op jit(solution)/shard_map/reshape | solution.py:582
  1.9 1.4 %copy.14.labels_ref = s32[128,1]{1,0:T(8,128)} copy(s32[128,1]{0,1:T(1,128)} %param.17) | data formatting | bytes 1024 | tf_op args[5]
  3.3 0.0 copy-start
  3.3 4.7 %copy.15.gate_hbm = bf16[4096,344]{1,0:T(8,128)(2,1)} copy(bf16[4096,344]{0,1:T(8,128)(2,1)} %param.21) | data formatting | bytes 5636096 | tf_op args[9]
  8.1 0.0 copy-done
  8.1 2.8 %copy.16.up_hbm = bf16[4096,344]{1,0:T(8,128)(2,1)} copy(bf16[4096,344]{0,1:T(8,128)(2,1)S(1)} %copy-done) | data formatting | bytes 5636096 | tf_op args[10]
  10.9 87.9 %shard_map.131 = (bf16[128,512]{1,0:T(8,128)(2,1)}, f32[1,8]{1,0:T(1,128)}) custom-call(s32[1,4]{1,0:T(1,128)} %lengths_ref.1, s32[128,1]{1,0:T(8,128)} %copy.14.labels_ref, f32[1,128]{1,0:T(1,128)} %bitcast.3, f32[1,8]{1,0:T(1,128)} %bitcast.4, f32[8,512]{1,0:T(8,128)} %reshape.18.gain_ref, bf16[128,512]{1,0:T(8,128)(2,1)} %res_hbm.1, ...), custom_call_target="tpu_custom_call" | custom-call | tf_op jit(solution)/shard_map/pallas_call | solution.py:529
  98.7 1.6 %copy.19 = bf16[128,512]{1,0:T(8,128)(2,1)} copy(bf16[128,512]{1,0:T(8,128)(2,1)} %get-tuple-element.8) | data formatting | bytes 262144
  100.3 1.1 %copy.20 = f32[8]{0:T(128)} copy(f32[8]{0:T(128)} %bitcast.5) | data formatting | bytes 64
Async XLA Ops:
  3.3 4.7 %copy-start = (bf16[4096,344]{0,1:T(8,128)(2,1)S(1)}, bf16[4096,344]{0,1:T(8,128)(2,1)}, u32[]{:S(2)}) copy-start(bf16[4096,344]{0,1:T(8,128)(2,1)} %param.22) | copy-start | bytes 8454148

commit v2 on v1

--- a/solution.py
+++ b/solution.py
@@ -20,6 +20,7 @@
 RIGHT, LEFT = 0, 1
 F32, BF16 = jnp.float32, jnp.bfloat16
 MESH = pl.DeviceIdType.MESH
+NT = (((1,), (1,)), ((), ()))
 
 dro_step = 0.5
 
@@ -82,8 +83,8 @@
 
     at0 = lax.broadcasted_iota(jnp.int32, (TOK, TOK), 0)
     at1 = lax.broadcasted_iota(jnp.int32, (TOK, TOK), 1)
-    label_col = labels_ref[...].astype(F32)
-    label_row = jnp.sum(jnp.where(at0 == at1, label_col, 0.0), axis=0, keepdims=True)
+    label_row = labels_ref[...].astype(F32)
+    label_col = jnp.sum(jnp.where(at0 == at1, label_row, 0.0), axis=1, keepdims=True)
     same = label_col == label_row
     rank_row = jnp.sum(jnp.where(same & (at0 < at1), 1.0, 0.0), axis=0, keepdims=True)
     rank_col = jnp.sum(jnp.where(same & (at1 < at0), 1.0, 0.0), axis=1, keepdims=True)
@@ -109,7 +110,7 @@
     for head in range(COLS // HEAD_DIM):
         cut = slice(head * HEAD_DIM, (head + 1) * HEAD_DIM)
         scores = lax.dot_general(
-            q_v[:, cut], k_v[:, cut], (((1,), (1,)), ((), ())), preferred_element_type=F32
+            q_v[:, cut], k_v[:, cut], NT, preferred_element_type=F32
         ) * HEAD_DIM ** (-0.5)
         scores = jnp.where(allowed, scores, -1e30)
         exp_scores = jnp.exp(scores - jnp.max(scores, axis=1, keepdims=True))
@@ -245,7 +246,7 @@
             rel = rels[0] if len(rels) == 1 else jnp.where(i == 0, rels[0], rels[1])
             s = slice_at(rel)
             at = pl.multiple_of(s * COLS, COLS)
-            gain = gain_ref[pl.ds(s, 1), :]
+            gain = gain_ref[:, pl.ds(at, COLS)]
             for start in rows_from:
                 here = pl.ds(pl.multiple_of(start, 16), BLOCK)
                 value = xb[s, here, :].astype(F32)
@@ -254,11 +255,11 @@
                     sq[:, :128] + sq[:, 128:256] + sq[:, 256:384] + sq[:, 384:]
                 )
                 scaled = (value * gain).astype(BF16)
-                acc_g[here, :] += jnp.dot(
-                    scaled, gate_v[pl.ds(at, COLS), :], preferred_element_type=F32
+                acc_g[here, :] += lax.dot_general(
+                    scaled, gate_v[:, pl.ds(at, COLS)], NT, preferred_element_type=F32
                 )
-                acc_u[here, :] += jnp.dot(
-                    scaled, up_v[pl.ds(at, COLS), :], preferred_element_type=F32
+                acc_u[here, :] += lax.dot_general(
+                    scaled, up_v[:, pl.ds(at, COLS)], NT, preferred_element_type=F32
                 )
             return carry
 
@@ -539,8 +540,8 @@
             pltpu.VMEM(tile, BF16),
             pltpu.VMEM(tile, BF16),
             pltpu.VMEM(tile, BF16),
-            pltpu.VMEM((NZ * COLS, HID), BF16),
-            pltpu.VMEM((NZ * COLS, HID), BF16),
+            pltpu.VMEM((HID, NZ * COLS), BF16),
+            pltpu.VMEM((HID, NZ * COLS), BF16),
             pltpu.VMEM((NZ, HID, COLS), BF16),
             pltpu.VMEM(tile, BF16),
             pltpu.VMEM((EXPERTS, PAD, COLS), BF16),
@@ -578,9 +579,9 @@
             collective_id=0, has_side_effects=True, vmem_limit_bytes=60 * 1024 * 1024
         ),
     )(
-        lengths, labels, losses.reshape(1, TOK), prior_weights.reshape(1, EXPERTS),
-        norm_gain.reshape(NZ, COLS), residual, queries, key_rows, value_rows,
-        gate_weight, up_weight, down_weight,
+        lengths, labels.reshape(1, TOK), losses.reshape(1, TOK), prior_weights.reshape(1, EXPERTS),
+        norm_gain.reshape(1, NZ * COLS), residual, queries, key_rows, value_rows,
+        gate_weight.T, up_weight.T, down_weight,
     )
     return (mixed, weights.reshape(EXPERTS))
 

time: 102 us -> 92.1 us (0.903)
  local copies, waits for them, and re-layouts: 12.9 us -> 2.74 us
    unnamed x7 -> x2, local copies, waits for them, and re-layouts: 11.6 us -> 2.74 us
    reshape x1 -> x0, local copies, waits for them, and re-layouts: 1.32 us -> none  [body(): norm_gain.reshape(NZ, COLS)]
where the time goes in v2:
time: 92.1 us; the launch traced here: 91.6 us
  Pallas kernels  88.2 us (96%)
  local copies, waits for them, and re-layouts  2.74 us (3%)
    pallas_call x1, Pallas kernels, body(): pl.pallas_call(kernel, out_shape=(jax.ShapeDtypeStruct(tile, BF16), jax.S...  88.2 us
    unnamed x2, local copies, waits for them, and re-layouts  2.74 us

profile of v2, /device:TPU:1, one launch (start us, length us, event | category | flops | bytes accessed | tf_op | source)
XLA Modules:
  0.0 91.6 jit_solution(6239472213312767651)
XLA Ops:
  0.6 88.2 %shard_map.131 = (bf16[128,512]{1,0:T(8,128)(2,1)}, f32[1,8]{1,0:T(1,128)}) custom-call(s32[1,4]{1,0:T(1,128)} %lengths_ref.1, s32[1,128]{1,0:T(1,128)} %bitcast.10, f32[1,128]{1,0:T(1,128)} %bitcast.11, f32[1,8]{1,0:T(1,128)} %bitcast.12, f32[1,4096]{1,0:T(1,128)} %bitcast.9, bf16[128,512]{1,0:T(8,128)(2,1)} %res_hbm.1, bf16[128,512]{1,0:T(8,128)(2,1)} %q_hbm.1, ...), custom_call_target="tpu_custom_call" | custom-call | tf_op jit(solution)/shard_map/pallas_call | solution.py:530
  88.8 1.6 %copy.16 = bf16[128,512]{1,0:T(8,128)(2,1)} copy(bf16[128,512]{1,0:T(8,128)(2,1)} %get-tuple-element.8) | data formatting | bytes 262144
  90.4 1.2 %copy.17 = f32[8]{0:T(128)} copy(f32[8]{0:T(128)} %bitcast.13) | data formatting | bytes 64

commit v3 on v2

v3 whole, which is shorter than its diff:
```python
import jax
import jax.numpy as jnp
from jax import lax
from jax.experimental import pallas as pl
from jax.experimental.pallas import tpu as pltpu
from jax.sharding import PartitionSpec as P

HEAD_DIM = 128
EXPERTS = 8
CAP = 24
TOK = 128
COLS = 512
HID = 344
HALF_N = 384
NZ = 8
CORE_ROWS = 16 * CAP
ROWS = 2 * CORE_ROWS
CHUNK = 4 * CAP
HALF = CHUNK // 2
WIDE = COLS // 2
SHARED = 2 * CHUNK
RIGHT, LEFT = 0, 1
F32, BF16 = jnp.float32, jnp.bfloat16
MESH = pl.DeviceIdType.MESH
NT = (((1,), (1,)), ((), ()))

dro_step = 0.5


def kernel(
    lengths_ref, labels_ref, losses_ref, prior_ref, gain_ref,
    res_hbm, q_hbm, k_hbm, v_hbm, gate_hbm, up_hbm, down_hbm,
    mixed_ref, weights_ref,
    res_v, q_v, k_v, v_v, gate_v, up_v, down_v, both_v,
    hidden, packed, stage, xb, acc, square, inner,
    part, sib_out, sib_in, ring_in, ring_out, y_out, y_in, ret_out, ret,
    stat_x, stat_y, stat_c, stat_src,
    in_sem, w_sem, a_send, a_recv, g_send, g_recv, gs_send, gs_recv, gy_send, gy_recv,
    rs_send, rs_recv, ry_send, ry_recv, r_send, r_recv, b_send, b_recv, st_send, st_recv,
):
    dp = lax.axis_index("dp")
    z = lax.axis_index("mp")
    core = lax.rem(dp, 2)
    xy = dp // 2
    x, y = xy // 4, lax.rem(xy, 4)
    yb = lax.rem(y, 2)

    def plane(tx, ty, tc=None):
        return ((tx * 4 + ty) * 2 + (core if tc is None else tc), z)

    sibling = (dp + 1 - 2 * core, z)
    partner = plane(x, y + 1 - 2 * yb)
    z_right = (dp, lax.rem(z + 1, NZ))
    z_left = (dp, lax.rem(z + NZ - 1, NZ))
    toward = (z_right, z_left)
    offsets = [((i // 4), i % 4) for i in range(1, 16)]

    barrier = pltpu.get_barrier_semaphore()
    peers = [plane(lax.rem(x + dx, 4), lax.rem(y + dy, 4)) for dx, dy in offsets]
    peers += [sibling, z_right, z_left]
    for peer in peers:
        pl.semaphore_signal(barrier, inc=1, device_id=peer, device_id_type=MESH)

    loads = [
        pltpu.make_async_copy(src, dst, in_sem.at[i])
        for i, (src, dst) in enumerate(((q_hbm, q_v), (k_hbm, k_v), (v_hbm, v_v), (res_hbm, res_v)))
    ]
    for load in loads:
        load.start()
    weight_loads = [
        pltpu.make_async_copy(gate_hbm, gate_v, w_sem.at[0]),
        pltpu.make_async_copy(up_hbm, up_v, w_sem.at[1]),
    ] + [
        pltpu.make_async_copy(down_hbm.at[:, pl.ds(i * COLS, COLS)], down_v.at[i], w_sem.at[2 + i])
        for i in range(NZ)
    ]
    for load in weight_loads:
        load.start()

    def remote(src, dst, send, recv, device):
        return pltpu.make_async_remote_copy(
            src_ref=src, dst_ref=dst, send_sem=send, recv_sem=recv,
            device_id=device, device_id_type=MESH,
        )

    at0 = lax.broadcasted_iota(jnp.int32, (TOK, TOK), 0)
    at1 = lax.broadcasted_iota(jnp.int32, (TOK, TOK), 1)
    label_row = labels_ref[...].astype(F32)
    label_col = jnp.sum(jnp.where(at0 == at1, label_row, 0.0), axis=1, keepdims=True)
    same = label_col == label_row
    rank_row = jnp.sum(jnp.where(same & (at0 < at1), 1.0, 0.0), axis=0, keepdims=True)
    rank_col = jnp.sum(jnp.where(same & (at1 < at0), 1.0, 0.0), axis=1, keepdims=True)
    slot_row = label_row * (2 * CAP) + rank_row
    slot_ids = lax.broadcasted_iota(jnp.int32, (EXPERTS * 2 * CAP, TOK), 0).astype(F32)
    select = [(slot_ids == slot_row + half * CAP).astype(BF16) for half in range(2)]

    domain = lax.broadcasted_iota(jnp.int32, (EXPERTS, TOK), 0).astype(F32)
    lane = lax.broadcasted_iota(jnp.int32, (EXPERTS, TOK), 1)
    member = (domain == label_row).astype(F32)
    loss_sum = jnp.sum(member * losses_ref[...], axis=1, keepdims=True)
    count = jnp.sum(member, axis=1, keepdims=True)
    stat_src[0] = jnp.where(lane == 0, loss_sum, jnp.where(lane == 1, count, 0.0))

    ends = [lengths_ref[0, 0]]
    for i in range(1, 4):
        ends.append(ends[-1] + lengths_ref[0, i])
    doc0 = sum((at0 >= end).astype(jnp.int32) for end in ends)
    doc1 = sum((at1 >= end).astype(jnp.int32) for end in ends)
    allowed = (doc0 == doc1) & (at1 <= at0)
    for load in loads:
        load.wait()
    for head in range(COLS // HEAD_DIM):
        cut = slice(head * HEAD_DIM, (head + 1) * HEAD_DIM)
        scores = lax.dot_general(
            q_v[:, cut], k_v[:, cut], NT, preferred_element_type=F32
        ) * HEAD_DIM ** (-0.5)
        scores = jnp.where(allowed, scores, -1e30)
        exp_scores = jnp.exp(scores - jnp.max(scores, axis=1, keepdims=True))
        probs = (exp_scores / jnp.sum(exp_scores, axis=1, keepdims=True)).astype(BF16)
        attn = jnp.dot(probs, v_v[:, cut], preferred_element_type=F32)
        hidden[:, cut] = (res_v[:, cut].astype(F32) + attn).astype(BF16)
    packed[...] = (
        (
            jnp.dot(select[0], hidden[:, :WIDE], preferred_element_type=F32)
            + jnp.dot(select[1], hidden[:, WIDE:], preferred_element_type=F32)
        )
        .astype(BF16)
        .reshape(EXPERTS, 2 * CAP, WIDE)
    )

    pl.semaphore_wait(barrier, len(peers))

    my_q = jnp.where(x >= 2, (x - 2) * 4 + y, 8 + y)

    def goes(ty):
        return (x >= 2) | (lax.rem(ty, 2) == x)

    def send_block(i):
        dx, dy = offsets[i]
        tx, ty = lax.rem(x + dx, 4), lax.rem(y + dy, 4)
        copy = remote(
            packed.at[2 * tx + ty // 2], stage.at[my_q], a_send.at[i], a_recv.at[my_q], plane(tx, ty)
        )
        return goes(ty), copy

    for i in range(15):
        allowed_i, copy = send_block(i)
        pl.when(allowed_i)(copy.start)

    @pl.when(goes(y))
    def _():
        stage[my_q] = packed[2 * x + y // 2]

    def seq_of(q):
        if q < 8:
            return 2 + q // 4, q % 4
        return yb, q - 8

    def stat_copy(i, phase):
        if phase == 0:
            dst, peer = stat_x, plane(lax.rem(x + i, 4), y)
            return remote(stat_src.at[0], dst.at[x], st_send.at[i - 1], st_recv.at[x], peer)
        if phase == 1:
            dst, peer = stat_y, plane(x, lax.rem(y + i, 4))
            return remote(stat_src.at[1], dst.at[y], st_send.at[2 + i], st_recv.at[4 + y], peer)
        return remote(stat_src.at[2], stat_c, st_send.at[6], st_recv.at[8], sibling)

    def stat_wait(i, phase):
        if phase == 0:
            at = lax.rem(x + i, 4)
            return remote(stat_src.at[0], stat_x.at[at], st_send.at[0], st_recv.at[at], plane(at, y))
        at = lax.rem(y + i, 4)
        return remote(stat_src.at[1], stat_y.at[at], st_send.at[0], st_recv.at[4 + at], plane(x, at))

    def stats(step):
        if step == 0:
            for i in range(1, 4):
                stat_copy(i, 0).start()
            stat_x[x] = stat_src[0]
        elif step == 1:
            for i in range(1, 4):
                stat_wait(i, 0).wait_recv()
            stat_src[1] = (stat_x[0] + stat_x[1]) + (stat_x[2] + stat_x[3])
            for i in range(1, 4):
                stat_copy(i, 1).start()
            stat_y[y] = stat_src[1]
        elif step == 2:
            for i in range(1, 4):
                stat_wait(i, 1).wait_recv()
            stat_src[2] = (stat_y[0] + stat_y[1]) + (stat_y[2] + stat_y[3])
            stat_copy(0, 2).start()
        else:
            stat_copy(0, 2).wait_recv()
            totals = stat_src[2] + stat_c[...]
            domain_mean = totals[:, 0:1] / totals[:, 1:2]
            eye = lax.broadcasted_iota(jnp.int32, (EXPERTS, EXPERTS), 0) == lax.broadcasted_iota(
                jnp.int32, (EXPERTS, EXPERTS), 1
            )
            mean_row = jnp.sum(jnp.where(eye, domain_mean, 0.0), axis=0, keepdims=True)
            scaled = prior_ref[...] * jnp.exp(dro_step * mean_row)
            weights_ref[...] = EXPERTS * scaled / jnp.sum(scaled, axis=1, keepdims=True)

    acc[...] = jnp.zeros_like(acc)
    square[...] = jnp.zeros_like(square)
    for i in range(16):
        @pl.when(jnp.logical_not(goes(i % 4)))
        def _():
            ret[i] = jnp.zeros((2 * CAP, WIDE), BF16)

    for load in weight_loads:
        load.wait()

    def turn(i, carry):
        at = pl.ds(pl.multiple_of(i * COLS, COLS), COLS)
        for half, source in enumerate((gate_v, up_v)):
            first = half * HALF_N
            both_v[at, first + HALF_N - 128:first + HALF_N] = jnp.zeros((COLS, 128), BF16)
            both_v[at, first:first + HID] = source[:, at].T
        return carry

    lax.fori_loop(0, NZ, turn, 0)

    own_off = SHARED + yb * CHUNK
    other_off = SHARED + (1 - yb) * CHUNK
    OWN, C0, C1, OTHER = 0, 1, 2, 3
    piece_off = (own_off, 0, CHUNK, other_off)
    b_first = 2 * SHARED
    own_at = (b_first + yb * CHUNK, 0, SHARED, b_first + (1 - yb) * CHUNK)
    sib_at = tuple(
        at + step for at, step in zip(own_at, (SHARED, CHUNK, CHUNK, SHARED), strict=True)
    )
    groups = {
        "a": (0, 2 * SHARED, 0, SHARED, (C0, C1)),
        "c0": (0, SHARED, 0, CHUNK, (C0,)),
        "c1": (SHARED, SHARED, CHUNK, CHUNK, (C1,)),
        "b": (b_first, 2 * SHARED, SHARED, SHARED, (OWN, OTHER)),
    }
    group_sem = {"a": 0, "c0": 0, "c1": 1, "b": 2}
    lanes = {"B": (OWN, OWN), "C0": (C0, C0), "C1": (C1, C1), "A0": (C0, C1), "A1": (C1, C0)}
    first_q = {C0: 0, C1: 4, OWN: 8}

    def slice_at(rel):
        return lax.rem(z + rel, NZ)

    def rel_of(way, distance):
        return distance if way == RIGHT else (NZ - distance) % NZ

    def rows_at(off, rows):
        if isinstance(off, int):
            return pl.ds(off, rows)
        return pl.ds(pl.multiple_of(off, 16), rows)

    def part_of(way, lane, distance):
        if distance < 4 or lane in ("A0", "A1"):
            return 0, CHUNK
        return way * HALF, HALF

    started = []

    def go(copy):
        copy.start()
        started.append(copy)

    def gather_copy(way, hop, lane, sending):
        rel = rel_of(1 - way, hop - 1 if sending else hop)
        piece = lanes[lane][way]
        first, rows = part_of(way, lane, hop)
        ref = xb.at[slice_at(rel), rows_at(own_at[piece] + first, rows)]
        at = (way, hop - 1, piece)
        return remote(ref, ref, g_send.at[at], g_recv.at[at], toward[way])

    def sib_copy(rel, piece):
        return remote(
            xb.at[slice_at(rel), rows_at(own_at[piece], CHUNK)],
            xb.at[slice_at(rel), rows_at(sib_at[piece], CHUNK)],
            gs_send.at[rel, piece], gs_recv.at[rel, piece], sibling,
        )

    def y_copy(rel, mine=True):
        ref = xb.at[slice_at(rel), rows_at(own_at[OWN if mine else OTHER], CHUNK)]
        return remote(ref, ref, gy_send.at[rel], gy_recv.at[rel], partner)

    def spread(rel, piece):
        if piece == OWN:
            go(y_copy(rel))
        go(sib_copy(rel, piece))

    def start(piece):
        first = first_q[piece]
        for q in range(first, first + 4):
            sx, sy = seq_of(q)
            arrival = remote(
                packed.at[0], stage.at[q], a_send.at[0], a_recv.at[q], plane(sx, sy)
            )
            pl.when((sx != x) | (sy != y))(arrival.wait_recv)
        blocks = stage[first:first + 4].astype(F32)
        here = rows_at(own_at[piece], CHUNK)
        for half in range(2):
            xb[z, here, half * WIDE:(half + 1) * WIDE] = (
                blocks[:, half * CAP:(half + 1) * CAP].reshape(CHUNK, WIDE).astype(BF16)
            )

    def first_hop(lane):
        for way in (RIGHT, LEFT):
            go(gather_copy(way, 1, lane, True))

    def own_spread(piece):
        spread(0, piece)

    def hop(lane, h):
        for way in (RIGHT, LEFT):
            gather_copy(way, h, lane, False).wait_recv()
            if h < 3 or (h == 3 and lane != "A1"):
                go(gather_copy(way, h + 1, lane, True))
        first, second = lanes[lane]
        if h == 4 and first == second:
            spread(4, first)
            return
        for way in (RIGHT, LEFT):
            spread(rel_of(1 - way, h), lanes[lane][way])

    def y_arrive(*rels):
        for rel in rels:
            y_copy(rel, mine=False).wait_recv()
            go(sib_copy(rel, OTHER))

    def multiply(group, *rels):
        first, rows, _, _, pieces = groups[group]
        here = pl.ds(first, rows)
        for rel in rels:
            for piece in pieces:
                sib_copy(rel, piece).wait_recv()
            s = slice_at(rel)
            at = pl.ds(pl.multiple_of(s * COLS, COLS), COLS)
            value = xb[s, here, :].astype(F32)
            sq = value * value
            square[here, :] += sq[:, :128] + sq[:, 128:256] + sq[:, 256:384] + sq[:, 384:]
            scaled = (value * gain_ref[:, at]).astype(BF16)
            acc[here, :] += jnp.dot(scaled, both_v[at, :], preferred_element_type=F32)

    def activate(group):
        first, rows = groups[group][:2]
        here = pl.ds(first, rows)
        mean = jnp.sum(square[here, :], axis=1, keepdims=True) * (1.0 / (NZ * COLS))
        scale = lax.rsqrt(mean + 1e-05)
        gate = acc[here, :HID] * scale
        up = acc[here, HALF_N:HALF_N + HID] * scale
        inner[here, :] = (gate / (1.0 + jnp.exp(-gate)) * up).astype(BF16)

    def rs_copy(group, rel):
        _, _, off, rows, _ = groups[group]
        here = pl.ds(off, rows)
        at = (rel, group_sem[group])
        return remote(
            sib_out.at[rel, here], sib_in.at[rel, here], rs_send.at[at], rs_recv.at[at], sibling
        )

    def ry_copy(rel):
        return remote(y_out.at[rel], y_in.at[rel], ry_send.at[rel], ry_recv.at[rel], partner)

    def prepare(group, *rels):
        first, rows, off, count, _ = groups[group]
        for rel in rels:
            value = jnp.dot(
                inner[first:first + rows, :], down_v[slice_at(rel)], preferred_element_type=F32
            )
            step = CHUNK if group != "b" else SHARED
            for i in range(0, count, step):
                part[rel, off + i:off + i + step] = value[2 * i:2 * i + step]
                sib_out[rel, off + i:off + i + step] = value[2 * i + step:2 * (i + step)].astype(BF16)
            go(rs_copy(group, rel))

    def join(group, *rels):
        _, _, off, count, _ = groups[group]
        for rel in rels:
            rs_copy(group, rel).wait_recv()
            if group != "b":
                here = slice(off, off + count)
                part[rel, here] += sib_in[rel, here].astype(F32)
                continue
            other = rows_at(other_off, CHUNK)
            y_out[rel] = (part[rel, other] + sib_in[rel, other].astype(F32)).astype(BF16)
            go(ry_copy(rel))
            own = rows_at(own_off, CHUNK)
            part[rel, own] += sib_in[rel, own].astype(F32)

    def y_join(*rels):
        own = rows_at(own_off, CHUNK)
        for rel in rels:
            ry_copy(rel).wait_recv()
            part[rel, own] += y_in[rel].astype(F32)

    def ring_copy(way, distance, lane):
        piece = lanes[lane][way]
        first, rows = part_of(way, lane, distance)
        here = rows_at(piece_off[piece] + first, rows)
        at = (way, distance - 1, piece)
        return remote(
            ring_out.at[way, distance - 1, here], ring_in.at[way, distance - 1, here],
            r_send.at[at], r_recv.at[at], toward[way],
        )

    def incoming(way, distance, lane):
        ring_copy(way, distance, lane).wait_recv()
        first, rows = part_of(way, lane, distance)
        here = rows_at(piece_off[lanes[lane][way]] + first, rows)
        return ring_in[way, distance - 1, here].astype(F32)

    def ring(lane, distance):
        for way in (RIGHT, LEFT):
            first, rows = part_of(way, lane, distance)
            here = rows_at(piece_off[lanes[lane][way]] + first, rows)
            value = part[rel_of(way, distance), here]
            if distance < 3 or (distance == 3 and lane == "A0"):
                value = value + incoming(way, distance + 1, lane)
            elif distance == 3 and lane != "A1":
                arrived = incoming(way, 4, lane)
                if way == RIGHT:
                    value = jnp.concatenate([value[:HALF] + arrived, value[HALF:]], axis=0)
                else:
                    value = jnp.concatenate([value[:HALF], value[HALF:] + arrived], axis=0)
            ring_out[way, distance - 1, here] = value.astype(BF16)
            go(ring_copy(way, distance, lane))

    def send_back(q):
        sx, sy = seq_of(q)
        return remote(ret_out.at[q], ret.at[xy], b_send.at[q], b_recv.at[xy], plane(sx, sy))

    def is_me(q):
        sx, sy = seq_of(q)
        return (sx == x) & (sy == y)

    def finish(piece):
        value = part[0, rows_at(piece_off[piece], CHUNK)]
        for way in (RIGHT, LEFT):
            lane = next(name for name in used if lanes[name][way] == piece)
            value = value + incoming(way, 1, lane)
        first = first_q[piece]
        ret_out[first:first + 4] = jnp.concatenate(
            [value[:, :WIDE].reshape(4, CAP, WIDE), value[:, WIDE:].reshape(4, CAP, WIDE)], axis=1
        ).astype(BF16)
        for q in range(first, first + 4):
            pl.when(jnp.logical_not(is_me(q)))(send_back(q).start)

    def drain():
        for copy in started:
            copy.wait_send()
        started.clear()

    used = ("B", "A0", "A1")
    start(OWN)
    first_hop("B")
    spread(0, OWN)
    start(C0)
    start(C1)
    first_hop("A0")
    spread(0, C0)
    spread(0, C1)
    stats(0)
    hop("B", 1)
    first_hop("A1")
    y_arrive(0)
    multiply("a", 0)
    hop("A0", 1)
    multiply("b", 0)
    hop("B", 2)
    y_arrive(1, 7)
    hop("A1", 1)
    stats(1)
    multiply("a", 1)
    hop("A0", 2)
    multiply("a", 7)
    hop("B", 3)
    multiply("b", 1)
    y_arrive(2, 6)
    hop("A1", 2)
    multiply("b", 7)
    stats(2)
    multiply("a", 2)
    hop("A0", 3)
    multiply("a", 6)
    hop("B", 4)
    y_arrive(3, 5)
    multiply("b", 2)
    hop("A1", 3)
    multiply("b", 6)
    multiply("a", 3)
    multiply("b", 3)
    hop("A0", 4)
    multiply("a", 5)
    multiply("a", 4)
    activate("a")
    prepare("a", 4)
    y_arrive(4)
    prepare("a", 3, 5)
    multiply("b", 5)
    join("a", 4)
    ring("A0", 4)
    multiply("b", 4)
    activate("b")
    prepare("b", 4)
    join("a", 3, 5)
    ring("A1", 3)
    prepare("b", 3, 5)
    join("b", 4, 3, 5)
    prepare("a", 2, 6)
    prepare("b", 2, 6)
    y_join(4)
    ring("B", 4)
    join("a", 2, 6)
    ring("A0", 3)
    join("b", 2, 6)
    y_join(3, 5)
    ring("B", 3)
    ring("A1", 2)
    prepare("a", 1, 7)
    prepare("b", 1, 7)
    join("a", 1, 7)
    ring("A0", 2)
    join("b", 1, 7)
    y_join(2, 6)
    ring("B", 2)
    ring("A1", 1)
    prepare("a", 0)
    prepare("b", 0)
    join("a", 0)
    ring("A0", 1)
    join("b", 0)
    y_join(1, 7)
    ring("B", 1)
    stats(3)
    y_join(0)
    finish(C0)
    finish(C1)
    finish(OWN)

    @pl.when(goes(y))
    def _():
        ret[xy] = ret_out[my_q]

    drain()
    for i in range(15):
        allowed_i, copy = send_block(i)
        pl.when(allowed_i)(copy.wait_send)
    for i in range(1, 4):
        stat_copy(i, 0).wait_send()
        stat_copy(i, 1).wait_send()
    stat_copy(0, 2).wait_send()

    place = lax.broadcasted_iota(jnp.int32, (TOK, 16 * 2 * CAP), 1).astype(F32)
    spot = label_col * (4 * CAP) + rank_col
    take = [
        ((place == spot + half * CAP) | (place == spot + (2 + half) * CAP)).astype(BF16)
        for half in range(2)
    ]
    for i in range(16):
        arrival = remote(
            ret_out.at[0], ret.at[i], b_send.at[0], b_recv.at[i], plane(i // 4, i % 4)
        )
        pl.when(goes(i % 4) & (xy != i))(arrival.wait_recv)
    returned = ret[...].reshape(16 * 2 * CAP, WIDE)
    for half in range(2):
        cut = slice(half * WIDE, (half + 1) * WIDE)
        expert_out = jnp.dot(take[half], returned, preferred_element_type=F32)
        mixed_ref[:, cut] = (hidden[:, cut].astype(F32) + expert_out).astype(BF16)
    for q in range(12):
        pl.when(jnp.logical_not(is_me(q)))(send_back(q).wait_send)


def body(
    residual, queries, key_rows, value_rows, lengths, labels, losses, prior_weights, norm_gain,
    gate_weight, up_weight, down_weight,
):
    vmem = pl.BlockSpec(memory_space=pltpu.VMEM)
    smem = pl.BlockSpec(memory_space=pltpu.SMEM)
    hbm = pl.BlockSpec(memory_space=pl.ANY)
    dma = pltpu.SemaphoreType.DMA
    tile = (TOK, COLS)
    mixed, weights = pl.pallas_call(
        kernel,
        out_shape=(
            jax.ShapeDtypeStruct(tile, BF16),
            jax.ShapeDtypeStruct((1, EXPERTS), F32),
        ),
        in_specs=[smem, vmem, vmem, vmem, vmem] + [hbm] * 7,
        out_specs=(vmem, vmem),
        scratch_shapes=[
            pltpu.VMEM(tile, BF16),
            pltpu.VMEM(tile, BF16),
            pltpu.VMEM(tile, BF16),
            pltpu.VMEM(tile, BF16),
            pltpu.VMEM((HID, NZ * COLS), BF16),
            pltpu.VMEM((HID, NZ * COLS), BF16),
            pltpu.VMEM((NZ, HID, COLS), BF16),
            pltpu.VMEM((NZ * COLS, 2 * HALF_N), BF16),
            pltpu.VMEM(tile, BF16),
            pltpu.VMEM((EXPERTS, 2 * CAP, WIDE), BF16),
            pltpu.VMEM((12, 2 * CAP, WIDE), BF16),
            pltpu.VMEM((NZ, ROWS, COLS), BF16),
            pltpu.VMEM((ROWS, 2 * HALF_N), F32),
            pltpu.VMEM((ROWS, 128), F32),
            pltpu.VMEM((ROWS, HID), BF16),
            pltpu.VMEM((NZ, CORE_ROWS, COLS), F32),
            pltpu.VMEM((NZ, CORE_ROWS, COLS), BF16),
            pltpu.VMEM((NZ, CORE_ROWS, COLS), BF16),
            pltpu.VMEM((2, 4, CORE_ROWS, COLS), BF16),
            pltpu.VMEM((2, 4, CORE_ROWS, COLS), BF16),
            pltpu.VMEM((NZ, CHUNK, COLS), BF16),
            pltpu.VMEM((NZ, CHUNK, COLS), BF16),
            pltpu.VMEM((12, 2 * CAP, WIDE), BF16),
            pltpu.VMEM((16, 2 * CAP, WIDE), BF16),
            pltpu.VMEM((4, EXPERTS, 128), F32),
            pltpu.VMEM((4, EXPERTS, 128), F32),
            pltpu.VMEM((EXPERTS, 128), F32),
            pltpu.VMEM((3, EXPERTS, 128), F32),
            dma((4,)), dma((2 + NZ,)),
            dma((15,)), dma((12,)),
            dma((2, 4, 3)), dma((2, 4, 3)),
            dma((NZ, 4)), dma((NZ, 4)),
            dma((NZ,)), dma((NZ,)),
            dma((NZ, 3)), dma((NZ, 3)),
            dma((NZ,)), dma((NZ,)),
            dma((2, 4, 3)), dma((2, 4, 3)),
            dma((12,)), dma((16,)),
            dma((7,)), dma((9,)),
        ],
        compiler_params=pltpu.CompilerParams(
            collective_id=0, has_side_effects=True, vmem_limit_bytes=60 * 1024 * 1024
        ),
    )(
        lengths, labels.reshape(1, TOK), losses.reshape(1, TOK), prior_weights.reshape(1, EXPERTS),
        norm_gain.reshape(1, NZ * COLS), residual, queries, key_rows, value_rows,
        gate_weight.T, up_weight.T, down_weight,
    )
    return (mixed, weights.reshape(EXPERTS))


def solution(mesh):
    placed = (
        P("dp", "mp"),
        P("dp", "mp"),
        P("dp", "mp"),
        P("dp", "mp"),
        P("dp", None),
        P("dp", None),
        P("dp"),
        P(),
        P(),
        P(None, ("dp", "mp")),
        P(None, ("dp", "mp")),
        P(("dp", "mp"), None),
    )
    return jax.shard_map(
        body, mesh=mesh, in_specs=placed, out_specs=(P("dp", "mp"), P()), check_vma=False
    )
```

time: 92.1 us -> 86.2 us (0.936)
  Pallas kernels: 88.2 us -> 81.9 us
    pallas_call x1, Pallas kernels: 88.2 us -> 81.9 us  [body(): pl.pallas_call(kernel, out_shape=(jax.ShapeDtypeStruct(tile, BF16), jax.S...]
where the time goes in v3:
time: 86.2 us; the launch traced here: 85.3 us
  Pallas kernels  81.9 us (95%)
  local copies, waits for them, and re-layouts  2.74 us (3%)
    pallas_call x1, Pallas kernels, body(): pl.pallas_call(kernel, out_shape=(jax.ShapeDtypeStruct(tile, BF16), jax.S...  81.9 us
    unnamed x2, local copies, waits for them, and re-layouts  2.74 us

profile of v3, /device:TPU:1, one launch (start us, length us, event | category | flops | bytes accessed | tf_op | source)
XLA Modules:
  0.0 85.3 jit_solution(13631424281978125094)
XLA Ops:
  0.6 81.9 %shard_map.131 = (bf16[128,512]{1,0:T(8,128)(2,1)}, f32[1,8]{1,0:T(1,128)}) custom-call(s32[1,4]{1,0:T(1,128)} %lengths_ref.1, s32[1,128]{1,0:T(1,128)} %bitcast.10, f32[1,128]{1,0:T(1,128)} %bitcast.11, f32[1,8]{1,0:T(1,128)} %bitcast.12, f32[1,4096]{1,0:T(1,128)} %bitcast.9, bf16[128,512]{1,0:T(8,128)(2,1)} %res_hbm.1, bf16[128,512]{1,0:T(8,128)(2,1)} %q_hbm.1, ...), custom_call_target="tpu_custom_call" | custom-call | tf_op jit(solution)/shard_map/pallas_call | solution.py:579
  82.5 1.6 %copy.16 = bf16[128,512]{1,0:T(8,128)(2,1)} copy(bf16[128,512]{1,0:T(8,128)(2,1)} %get-tuple-element.8) | data formatting | bytes 262144
  84.1 1.2 %copy.17 = f32[8]{0:T(128)} copy(f32[8]{0:T(128)} %bitcast.13) | data formatting | bytes 64

commit v4 on v3

--- a/solution.py
+++ b/solution.py
@@ -28,9 +28,10 @@
 
 
 def kernel(
-    lengths_ref, labels_ref, losses_ref, prior_ref, gain_ref,
+    lengths_hbm, labels_hbm, losses_hbm, prior_hbm, gain_hbm,
     res_hbm, q_hbm, k_hbm, v_hbm, gate_hbm, up_hbm, down_hbm,
     mixed_ref, weights_ref,
+    lengths_ref, labels_ref, losses_ref, prior_ref, gain_ref,
     res_v, q_v, k_v, v_v, gate_v, up_v, down_v, both_v,
     hidden, packed, stage, xb, acc, square, inner,
     part, sib_out, sib_in, ring_in, ring_out, y_out, y_in, ret_out, ret,
@@ -53,7 +54,10 @@
     z_right = (dp, lax.rem(z + 1, NZ))
     z_left = (dp, lax.rem(z + NZ - 1, NZ))
     toward = (z_right, z_left)
-    offsets = [((i // 4), i % 4) for i in range(1, 16)]
+    offsets = sorted(
+        ((i // 4, i % 4) for i in range(1, 16)),
+        key=lambda o: -(min(o[0], 4 - o[0]) + min(o[1], 4 - o[1])),
+    )
 
     barrier = pltpu.get_barrier_semaphore()
     peers = [plane(lax.rem(x + dx, 4), lax.rem(y + dy, 4)) for dx, dy in offsets]
@@ -63,7 +67,11 @@
 
     loads = [
         pltpu.make_async_copy(src, dst, in_sem.at[i])
-        for i, (src, dst) in enumerate(((q_hbm, q_v), (k_hbm, k_v), (v_hbm, v_v), (res_hbm, res_v)))
+        for i, (src, dst) in enumerate((
+            (labels_hbm, labels_ref), (lengths_hbm, lengths_ref), (losses_hbm, losses_ref),
+            (q_hbm, q_v), (k_hbm, k_v), (v_hbm, v_v), (res_hbm, res_v),
+            (prior_hbm, prior_ref), (gain_hbm, gain_ref),
+        ))
     ]
     for load in loads:
         load.start()
@@ -83,6 +91,9 @@
             device_id=device, device_id_type=MESH,
         )
 
+    for load in loads:
+        load.wait()
+
     at0 = lax.broadcasted_iota(jnp.int32, (TOK, TOK), 0)
     at1 = lax.broadcasted_iota(jnp.int32, (TOK, TOK), 1)
     label_row = labels_ref[...].astype(F32)
@@ -107,8 +118,6 @@
     doc0 = sum((at0 >= end).astype(jnp.int32) for end in ends)
     doc1 = sum((at1 >= end).astype(jnp.int32) for end in ends)
     allowed = (doc0 == doc1) & (at1 <= at0)
-    for load in loads:
-        load.wait()
     for head in range(COLS // HEAD_DIM):
         cut = slice(head * HEAD_DIM, (head + 1) * HEAD_DIM)
         scores = lax.dot_general(
@@ -130,10 +139,11 @@
 
     pl.semaphore_wait(barrier, len(peers))
 
-    my_q = jnp.where(x >= 2, (x - 2) * 4 + y, 8 + y)
+    kind = lax.rem(x + y, 4)
+    my_q = jnp.where(kind >= 2, (kind - 2) * 4 + y, 8 + y)
 
     def goes(ty):
-        return (x >= 2) | (lax.rem(ty, 2) == x)
+        return (kind >= 2) | (lax.rem(ty, 2) == kind)
 
     def send_block(i):
         dx, dy = offsets[i]
@@ -152,9 +162,10 @@
         stage[my_q] = packed[2 * x + y // 2]
 
     def seq_of(q):
+        sy = q % 4
         if q < 8:
-            return 2 + q // 4, q % 4
-        return yb, q - 8
+            return (2 + q // 4 - sy) % 4, sy
+        return lax.rem(yb - sy + 4, 4), sy
 
     def stat_copy(i, phase):
         if phase == 0:
@@ -225,18 +236,9 @@
     OWN, C0, C1, OTHER = 0, 1, 2, 3
     piece_off = (own_off, 0, CHUNK, other_off)
     b_first = 2 * SHARED
-    own_at = (b_first + yb * CHUNK, 0, SHARED, b_first + (1 - yb) * CHUNK)
-    sib_at = tuple(
-        at + step for at, step in zip(own_at, (SHARED, CHUNK, CHUNK, SHARED), strict=True)
-    )
-    groups = {
-        "a": (0, 2 * SHARED, 0, SHARED, (C0, C1)),
-        "c0": (0, SHARED, 0, CHUNK, (C0,)),
-        "c1": (SHARED, SHARED, CHUNK, CHUNK, (C1,)),
-        "b": (b_first, 2 * SHARED, SHARED, SHARED, (OWN, OTHER)),
-    }
-    group_sem = {"a": 0, "c0": 0, "c1": 1, "b": 2}
-    lanes = {"B": (OWN, OWN), "C0": (C0, C0), "C1": (C1, C1), "A0": (C0, C1), "A1": (C1, C0)}
+    own_at = (b_first + yb * CHUNK, 0, CHUNK, b_first + (1 - yb) * CHUNK)
+    groups = {"a": (0, 0, 0), "b": (b_first, SHARED, 1)}
+    lanes = {"B": (OWN, OWN), "A0": (C0, C1), "A1": (C1, C0)}
     first_q = {C0: 0, C1: 4, OWN: 8}
 
     def slice_at(rel):
@@ -269,12 +271,16 @@
         at = (way, hop - 1, piece)
         return remote(ref, ref, g_send.at[at], g_recv.at[at], toward[way])
 
-    def sib_copy(rel, piece):
+    def sib_copy(group, rel):
+        first, _, number = groups[group]
+        rows = xb.at[slice_at(rel)]
         return remote(
-            xb.at[slice_at(rel), rows_at(own_at[piece], CHUNK)],
-            xb.at[slice_at(rel), rows_at(sib_at[piece], CHUNK)],
-            gs_send.at[rel, piece], gs_recv.at[rel, piece], sibling,
+            rows.at[pl.ds(first, SHARED)], rows.at[pl.ds(first + SHARED, SHARED)],
+            gs_send.at[rel, number], gs_recv.at[rel, number], sibling,
         )
+
+    def share(group, rel):
+        go(sib_copy(group, rel))
 
     def y_copy(rel, mine=True):
         ref = xb.at[slice_at(rel), rows_at(own_at[OWN if mine else OTHER], CHUNK)]
@@ -283,7 +289,6 @@
     def spread(rel, piece):
         if piece == OWN:
             go(y_copy(rel))
-        go(sib_copy(rel, piece))
 
     def start(piece):
         first = first_q[piece]
@@ -322,14 +327,12 @@
     def y_arrive(*rels):
         for rel in rels:
             y_copy(rel, mine=False).wait_recv()
-            go(sib_copy(rel, OTHER))
+            share("b", rel)
 
     def multiply(group, *rels):
-        first, rows, _, _, pieces = groups[group]
-        here = pl.ds(first, rows)
+        here = pl.ds(groups[group][0], 2 * SHARED)
         for rel in rels:
-            for piece in pieces:
-                sib_copy(rel, piece).wait_recv()
+            sib_copy(group, rel).wait_recv()
             s = slice_at(rel)
             at = pl.ds(pl.multiple_of(s * COLS, COLS), COLS)
             value = xb[s, here, :].astype(F32)
@@ -339,8 +342,7 @@
             acc[here, :] += jnp.dot(scaled, both_v[at, :], preferred_element_type=F32)
 
     def activate(group):
-        first, rows = groups[group][:2]
-        here = pl.ds(first, rows)
+        here = pl.ds(groups[group][0], 2 * SHARED)
         mean = jnp.sum(square[here, :], axis=1, keepdims=True) * (1.0 / (NZ * COLS))
         scale = lax.rsqrt(mean + 1e-05)
         gate = acc[here, :HID] * scale
@@ -348,9 +350,9 @@
         inner[here, :] = (gate / (1.0 + jnp.exp(-gate)) * up).astype(BF16)
 
     def rs_copy(group, rel):
-        _, _, off, rows, _ = groups[group]
-        here = pl.ds(off, rows)
-        at = (rel, group_sem[group])
+        _, off, number = groups[group]
+        here = pl.ds(off, SHARED)
+        at = (rel, number)
         return remote(
             sib_out.at[rel, here], sib_in.at[rel, here], rs_send.at[at], rs_recv.at[at], sibling
         )
@@ -359,24 +361,20 @@
         return remote(y_out.at[rel], y_in.at[rel], ry_send.at[rel], ry_recv.at[rel], partner)
 
     def prepare(group, *rels):
-        first, rows, off, count, _ = groups[group]
+        first, off, _ = groups[group]
         for rel in rels:
             value = jnp.dot(
-                inner[first:first + rows, :], down_v[slice_at(rel)], preferred_element_type=F32
+                inner[first:first + 2 * SHARED, :], down_v[slice_at(rel)], preferred_element_type=F32
             )
-            step = CHUNK if group != "b" else SHARED
-            for i in range(0, count, step):
-                part[rel, off + i:off + i + step] = value[2 * i:2 * i + step]
-                sib_out[rel, off + i:off + i + step] = value[2 * i + step:2 * (i + step)].astype(BF16)
+            sib_out[rel, off:off + SHARED] = value[SHARED:].astype(BF16)
+            part[rel, off:off + SHARED] = value[:SHARED]
             go(rs_copy(group, rel))
 
     def join(group, *rels):
-        _, _, off, count, _ = groups[group]
         for rel in rels:
             rs_copy(group, rel).wait_recv()
-            if group != "b":
-                here = slice(off, off + count)
-                part[rel, here] += sib_in[rel, here].astype(F32)
+            if group == "a":
+                part[rel, :SHARED] += sib_in[rel, :SHARED].astype(F32)
                 continue
             other = rows_at(other_off, CHUNK)
             y_out[rel] = (part[rel, other] + sib_in[rel, other].astype(F32)).astype(BF16)
@@ -449,89 +447,113 @@
 
     used = ("B", "A0", "A1")
     start(OWN)
+    spread(0, OWN)
     first_hop("B")
-    spread(0, OWN)
     start(C0)
+    spread(0, C0)
     start(C1)
+    spread(0, C1)
     first_hop("A0")
-    spread(0, C0)
-    spread(0, C1)
+    share("a", 0)
+    first_hop("A1")
+    multiply("a", 0)
+    y_arrive(0)
+    hop("B", 1)
     stats(0)
-    hop("B", 1)
-    first_hop("A1")
-    y_arrive(0)
-    multiply("a", 0)
+    multiply("b", 0)
     hop("A0", 1)
-    multiply("b", 0)
+    hop("A1", 1)
+    share("a", 1)
+    share("a", 7)
+    multiply("a", 1)
     hop("B", 2)
+    stats(1)
+    multiply("a", 7)
     y_arrive(1, 7)
-    hop("A1", 1)
-    stats(1)
-    multiply("a", 1)
     hop("A0", 2)
-    multiply("a", 7)
+    multiply("b", 1)
+    multiply("b", 7)
+    hop("A1", 2)
+    share("a", 2)
+    share("a", 6)
+    multiply("a", 2)
     hop("B", 3)
-    multiply("b", 1)
+    multiply("a", 6)
     y_arrive(2, 6)
-    hop("A1", 2)
-    multiply("b", 7)
+    hop("A0", 3)
+    multiply("b", 2)
+    multiply("b", 6)
+    hop("A1", 3)
+    share("a", 5)
+    share("a", 3)
+    hop("B", 4)
     stats(2)
-    multiply("a", 2)
-    hop("A0", 3)
-    multiply("a", 6)
-    hop("B", 4)
+    multiply("a", 5)
+    multiply("a", 3)
+    hop("A0", 4)
+    share("a", 4)
     y_arrive(3, 5)
-    multiply("b", 2)
-    hop("A1", 3)
-    multiply("b", 6)
-    multiply("a", 3)
-    multiply("b", 3)
-    hop("A0", 4)
-    multiply("a", 5)
     multiply("a", 4)
     activate("a")
+    prepare("a", 3)
+    y_arrive(4)
     prepare("a", 4)
-    y_arrive(4)
-    prepare("a", 3, 5)
+    multiply("b", 3)
     multiply("b", 5)
-    join("a", 4)
-    ring("A0", 4)
     multiply("b", 4)
     activate("b")
     prepare("b", 4)
-    join("a", 3, 5)
+    prepare("b", 6)
+    join("a", 3)
+    prepare("b", 3)
+    join("a", 4)
+    join("b", 4)
+    ring("A0", 4)
+    prepare("a", 5)
+    join("b", 3)
+    prepare("a", 7)
+    prepare("b", 5)
+    join("a", 5)
     ring("A1", 3)
-    prepare("b", 3, 5)
-    join("b", 4, 3, 5)
-    prepare("a", 2, 6)
-    prepare("b", 2, 6)
+    prepare("a", 6)
+    join("a", 7)
+    join("b", 5)
+    prepare("a", 2)
+    join("b", 6)
     y_join(4)
     ring("B", 4)
-    join("a", 2, 6)
     ring("A0", 3)
-    join("b", 2, 6)
-    y_join(3, 5)
+    join("a", 2)
+    prepare("b", 7)
+    prepare("b", 2)
+    prepare("a", 0)
+    join("a", 6)
+    ring("A1", 2)
+    join("b", 7)
+    join("b", 2)
+    y_join(5)
+    join("a", 0)
+    y_join(3)
     ring("B", 3)
-    ring("A1", 2)
-    prepare("a", 1, 7)
-    prepare("b", 1, 7)
-    join("a", 1, 7)
+    prepare("a", 1)
+    prepare("b", 0)
+    y_join(6)
+    prepare("b", 1)
     ring("A0", 2)
-    join("b", 1, 7)
-    y_join(2, 6)
+    join("a", 1)
+    join("b", 0)
+    join("b", 1)
+    ring("A1", 1)
+    y_join(7)
+    y_join(2)
     ring("B", 2)
-    ring("A1", 1)
-    prepare("a", 0)
-    prepare("b", 0)
-    join("a", 0)
     ring("A0", 1)
-    join("b", 0)
-    y_join(1, 7)
+    y_join(0)
+    y_join(1)
     ring("B", 1)
     stats(3)
-    y_join(0)
+    finish(C1)
     finish(C0)
-    finish(C1)
     finish(OWN)
 
     @pl.when(goes(y))
@@ -567,12 +589,16 @@
         pl.when(jnp.logical_not(is_me(q)))(send_back(q).wait_send)
 
 
+def hand_on(mixed_in, weights_in, mixed_out, weights_out):
+    mixed_out[...] = mixed_in[...]
+    weights_out[...] = weights_in[...]
+
+
 def body(
     residual, queries, key_rows, value_rows, lengths, labels, losses, prior_weights, norm_gain,
     gate_weight, up_weight, down_weight,
 ):
     vmem = pl.BlockSpec(memory_space=pltpu.VMEM)
-    smem = pl.BlockSpec(memory_space=pltpu.SMEM)
     hbm = pl.BlockSpec(memory_space=pl.ANY)
     dma = pltpu.SemaphoreType.DMA
     tile = (TOK, COLS)
@@ -582,9 +608,14 @@
             jax.ShapeDtypeStruct(tile, BF16),
             jax.ShapeDtypeStruct((1, EXPERTS), F32),
         ),
-        in_specs=[smem, vmem, vmem, vmem, vmem] + [hbm] * 7,
+        in_specs=[hbm] * 12,
         out_specs=(vmem, vmem),
         scratch_shapes=[
+            pltpu.SMEM((1, 4), jnp.int32),
+            pltpu.VMEM((1, TOK), jnp.int32),
+            pltpu.VMEM((1, TOK), F32),
+            pltpu.VMEM((1, EXPERTS), F32),
+            pltpu.VMEM((1, NZ * COLS), F32),
             pltpu.VMEM(tile, BF16),
             pltpu.VMEM(tile, BF16),
             pltpu.VMEM(tile, BF16),
@@ -613,12 +644,12 @@
             pltpu.VMEM((4, EXPERTS, 128), F32),
             pltpu.VMEM((EXPERTS, 128), F32),
             pltpu.VMEM((3, EXPERTS, 128), F32),
-            dma((4,)), dma((2 + NZ,)),
+            dma((9,)), dma((2 + NZ,)),
             dma((15,)), dma((12,)),
             dma((2, 4, 3)), dma((2, 4, 3)),
-            dma((NZ, 4)), dma((NZ, 4)),
+            dma((NZ, 2)), dma((NZ, 2)),
             dma((NZ,)), dma((NZ,)),
-            dma((NZ, 3)), dma((NZ, 3)),
+            dma((NZ, 2)), dma((NZ, 2)),
             dma((NZ,)), dma((NZ,)),
             dma((2, 4, 3)), dma((2, 4, 3)),
             dma((12,)), dma((16,)),
@@ -632,6 +663,15 @@
         norm_gain.reshape(1, NZ * COLS), residual, queries, key_rows, value_rows,
         gate_weight.T, up_weight.T, down_weight,
     )
+    mixed, weights = pl.pallas_call(
+        hand_on,
+        out_shape=(
+            jax.ShapeDtypeStruct(tile, BF16),
+            jax.ShapeDtypeStruct((1, EXPERTS), F32),
+        ),
+        in_specs=[vmem, vmem],
+        out_specs=(vmem, vmem),
+    )(mixed, weights)
     return (mixed, weights.reshape(EXPERTS))
 
 

time: 86.2 us -> 82.2 us (0.954)
  local copies, waits for them, and re-layouts: 2.74 us -> 0 us
    unnamed x2 -> x0, local copies, waits for them, and re-layouts: 2.74 us -> none
    pallas_call x1, Pallas kernels: 81.9 us -> 79.8 us  [body(): pl.pallas_call(kernel, out_shape=(jax.ShapeDtypeStruct(tile, BF16), jax.S...]
    pallas_call x0 -> x1, Pallas kernels: none -> 1.57 us  [body(): pl.pallas_call(hand_on, out_shape=(jax.ShapeDtypeStruct(tile, BF16), jax....]
where the time goes in v4:
time: 82.2 us; the launch traced here: 82.1 us
  Pallas kernels  81.4 us (99%)
    pallas_call x1, Pallas kernels, body(): pl.pallas_call(kernel, out_shape=(jax.ShapeDtypeStruct(tile, BF16), jax.S...  79.8 us

profile of v4, /device:TPU:1, one launch (start us, length us, event | category | flops | bytes accessed | tf_op | source)
XLA Modules:
  0.0 82.1 jit_solution(3949189809503602083)
XLA Ops:
  0.6 79.8 %shard_map.131 = (bf16[128,512]{1,0:T(8,128)(2,1)}, f32[1,8]{1,0:T(1,128)}) custom-call(s32[1,4]{1,0:T(1,128)} %lengths_hbm.1, s32[1,128]{1,0:T(1,128)} %bitcast.10, f32[1,128]{1,0:T(1,128)} %bitcast.11, f32[1,8]{1,0:T(1,128)} %bitcast.12, f32[1,4096]{1,0:T(1,128)} %bitcast.9, bf16[128,512]{1,0:T(8,128)(2,1)} %res_hbm.1, bf16[128,512]{1,0:T(8,128)(2,1)} %q_hbm.1, ...), custom_call_target="tpu_custom_call" | custom-call | tf_op jit(solution)/shard_map/pallas_call | solution.py:605
  80.5 1.6 %shard_map.132 = (bf16[128,512]{1,0:T(8,128)(2,1)}, f32[1,8]{1,0:T(1,128)}) custom-call(bf16[128,512]{1,0:T(8,128)(2,1)} %get-tuple-element.6.mixed_in, f32[1,8]{1,0:T(1,128)} %get-tuple-element.7.weights_in), custom_call_target="tpu_custom_call" | custom-call | tf_op jit(solution)/shard_map/pallas_call | solution.py:666

commit v5 on v4

--- a/solution.py
+++ b/solution.py
@@ -440,10 +440,10 @@
         for q in range(first, first + 4):
             pl.when(jnp.logical_not(is_me(q)))(send_back(q).start)
 
-    def drain():
-        for copy in started:
+    def retire(count):
+        for copy in started[:count]:
             copy.wait_send()
-        started.clear()
+        del started[:count]
 
     used = ("B", "A0", "A1")
     start(OWN)
@@ -522,32 +522,46 @@
     join("b", 6)
     y_join(4)
     ring("B", 4)
+    retire(12)
     ring("A0", 3)
+    retire(12)
     join("a", 2)
     prepare("b", 7)
     prepare("b", 2)
     prepare("a", 0)
     join("a", 6)
     ring("A1", 2)
+    retire(12)
     join("b", 7)
     join("b", 2)
     y_join(5)
     join("a", 0)
     y_join(3)
     ring("B", 3)
+    retire(12)
     prepare("a", 1)
     prepare("b", 0)
     y_join(6)
     prepare("b", 1)
     ring("A0", 2)
+    retire(12)
     join("a", 1)
     join("b", 0)
     join("b", 1)
     ring("A1", 1)
+    for i in range(15):
+        allowed_i, copy = send_block(i)
+        pl.when(allowed_i)(copy.wait_send)
+    for i in range(1, 4):
+        stat_copy(i, 0).wait_send()
+        stat_copy(i, 1).wait_send()
+    stat_copy(0, 2).wait_send()
     y_join(7)
     y_join(2)
     ring("B", 2)
+    retire(16)
     ring("A0", 1)
+    retire(8)
     y_join(0)
     y_join(1)
     ring("B", 1)
@@ -560,14 +574,7 @@
     def _():
         ret[xy] = ret_out[my_q]
 
-    drain()
-    for i in range(15):
-        allowed_i, copy = send_block(i)
-        pl.when(allowed_i)(copy.wait_send)
-    for i in range(1, 4):
-        stat_copy(i, 0).wait_send()
-        stat_copy(i, 1).wait_send()
-    stat_copy(0, 2).wait_send()
+    retire(len(started))
 
     place = lax.broadcasted_iota(jnp.int32, (TOK, 16 * 2 * CAP), 1).astype(F32)
     spot = label_col * (4 * CAP) + rank_col

time: 82.2 us -> 82.2 us (level)
  no operation moved by 1% of the time
where the time goes in v5:
time: 82.2 us; the launch traced here: 82.1 us
  Pallas kernels  81.4 us (99%)
    pallas_call x1, Pallas kernels, body(): pl.pallas_call(kernel, out_shape=(jax.ShapeDtypeStruct(tile, BF16), jax.S...  79.9 us

profile of v5, /device:TPU:1, one launch (start us, length us, event | category | flops | bytes accessed | tf_op | source)
XLA Modules:
  0.0 82.1 jit_solution(7917325394067572512)
XLA Ops:
  0.6 79.9 %shard_map.131 = (bf16[128,512]{1,0:T(8,128)(2,1)}, f32[1,8]{1,0:T(1,128)}) custom-call(s32[1,4]{1,0:T(1,128)} %lengths_hbm.1, s32[1,128]{1,0:T(1,128)} %bitcast.10, f32[1,128]{1,0:T(1,128)} %bitcast.11, f32[1,8]{1,0:T(1,128)} %bitcast.12, f32[1,4096]{1,0:T(1,128)} %bitcast.9, bf16[128,512]{1,0:T(8,128)(2,1)} %res_hbm.1, bf16[128,512]{1,0:T(8,128)(2,1)} %q_hbm.1, ...), custom_call_target="tpu_custom_call" | custom-call | tf_op jit(solution)/shard_map/pallas_call | solution.py:612
  80.5 1.6 %shard_map.132 = (bf16[128,512]{1,0:T(8,128)(2,1)}, f32[1,8]{1,0:T(1,128)}) custom-call(bf16[128,512]{1,0:T(8,128)(2,1)} %get-tuple-element.6.mixed_in, f32[1,8]{1,0:T(1,128)} %get-tuple-element.7.weights_in), custom_call_target="tpu_custom_call" | custom-call | tf_op jit(solution)/shard_map/pallas_call | solution.py:673
